TPU v7x, 128 devices: a whole 4x4x4 slice. The times are simulated.
128 devices in a mesh: grp: 4 (over y_hi, core), st: 32 (over z, y_lo, x).
Axes of the slice: x: 4, y: 4 (y_hi: 2, y_lo: 2; y = y_hi * 2 + y_lo), z: 4, core: 2. Of those that a mesh axis runs over, the one named last changes fastest.
Arguments:
- start_vectors: float32 [32, 131072], P(None, ('grp', 'st')), may hold values from -6 to 6
- stay: float32 [131072], P(('grp', 'st')), may hold values from 0.1 to 0.6
- band_blocks: bfloat16 [131072, 8192], P(('grp', 'st')), may hold values from 0.0009994507 to 1
- band_start: int32 [512], P(('grp', 'st')), may hold values from -4096 to 126976, as said below
- band_width: int32 [512], P(('grp', 'st')), may hold values from 4096 to 8192, as said below
Outputs:
- vectors: float32 [32, 131072], P(None, ('grp', 'st'))
- ritz: float32 [32, 32], replicated
Inputs may be any that keep to these rules, and one draw needn't show every extreme that they name: For band block b, band_start[b] - (b * 256 // 1024 - 4) * 1024 is a multiple of 128 from 0 to 1024; both ends occur in every draw. `band_width`: A multiple of 128; both ends occur in every draw.
All inputs are finite; a program needn't handle non-finite values.
Results may differ from a plain program's by a relative error of at most 0.0011.
Values may be sent and summed in bfloat16 or wider, within the bound.
A program may use at most 64 MiB of HBM per device.

v0:
```python
import jax
import jax.numpy as jnp
from jax import lax
from jax.sharding import PartitionSpec as P

ITERS = 12


def shifted(shard, axis, by):
    length = lax.axis_size(axis)
    pairs = [(i, i + by) for i in range(length) if 0 <= i + by < length]
    return lax.ppermute(shard, axis, pairs)


def band_terms(extended, relative, band_width, shaped):
    vector_count = extended.shape[0]
    band_span = shaped.shape[2]

    def take_window(offset):
        return lax.dynamic_slice_in_dim(extended, offset, band_span, 1)

    windows = jax.vmap(take_window)(relative)
    columns = lax.broadcasted_iota(jnp.int32, (1, 1, band_span), 2)
    windows = jnp.where(columns < band_width[:, None, None], windows, jnp.zeros((), jnp.bfloat16))
    terms = jnp.einsum("nkw,nrw->nkr", windows, shaped, preferred_element_type=jnp.float32)
    return jnp.transpose(terms, (1, 0, 2)).reshape(vector_count, -1)


def shards(start_vectors, stay, band_blocks, band_start, band_width):
    vector_count, row_count = start_vectors.shape
    band_span = band_blocks.shape[1]
    reach_dev = band_span // (2 * row_count)
    block_count = band_start.shape[0]
    shaped = band_blocks.reshape(block_count, row_count // block_count, band_span)
    members = lax.axis_size("st")
    states = row_count * members * lax.axis_size("grp")
    chain_index = lax.axis_index("grp") * members + lax.axis_index("st")
    relative = band_start - (chain_index - reach_dev) * row_count
    columns = lax.broadcasted_iota(jnp.int32, (1, 1, band_span), 2)
    kept = jnp.where(
        columns < band_width[:, None, None], shaped.astype(jnp.float32), jnp.float32(0.0)
    )
    rowsum = jnp.sum(kept, axis=2).reshape(row_count)
    leave_scale = (1.0 - stay) / rowsum

    def one_step(step_index, state_pair):
        current, ritz_matrix = state_pair
        rounded = current.astype(jnp.bfloat16)
        pieces = []
        for offset in range(-reach_dev, reach_dev + 1):
            if offset == 0:
                pieces.append(rounded)
            else:
                pieces.append(shifted(rounded, ("grp", "st"), -offset))
        extended = jnp.concatenate(pieces, axis=1)
        image = stay * current + leave_scale * band_terms(extended, relative, band_width, shaped)
        gram_local = jnp.dot(image, image.T, precision=lax.Precision.HIGHEST)
        cross_local = jnp.dot(current, image.T, precision=lax.Precision.HIGHEST)
        gram_matrix, cross_matrix = lax.psum((gram_local, cross_local), ("grp", "st"))
        gram_matrix = gram_matrix / states
        cross_matrix = cross_matrix / states
        lower_factor = jnp.linalg.cholesky(gram_matrix)
        updated = lax.linalg.triangular_solve(lower_factor, image, left_side=True, lower=True)
        return (updated, cross_matrix)

    ritz_start = jnp.zeros((vector_count, vector_count), jnp.float32)
    vectors, ritz_matrix = lax.fori_loop(0, ITERS, one_step, (start_vectors, ritz_start))
    return (vectors, ritz_matrix)


def solution(mesh):
    placed = (
        P(None, ("grp", "st")),
        P(("grp", "st")),
        P(("grp", "st"), None),
        P(("grp", "st")),
        P(("grp", "st")),
    )
    return jax.shard_map(
        shards, mesh=mesh, in_specs=placed, out_specs=(P(None, ("grp", "st")), P()), check_vma=False
    )
```

profile of v0, /device:TPU:1, one launch (start us, length us, event | category | flops | bytes accessed | tf_op | source)
XLA Modules:
  0.0 1466.9 jit_solution(9413725356419280123)
XLA Ops:
  9.6 1455.8 %while.18 = (s32[]{:T(128)}, f32[32,1024]{1,0:T(8,128)S(1)}, f32[32,32]{0,1:T(8,128)}, f32[1024]{0:T(1024)S(1)}, f32[1024]{0:T(1024)S(1)}, /*index=5*/s32[4]{0:T...) while((s32[]{:T(128)}, f32[32,1024]{1,0:T(8,128)S(1)}, ...), condition=%wide.region_6.7_spmd.clone, body=%wide.region_1.6_spmd.sunk.clone | while | flops 576075840 | bytes 25203616 | solution.py:67
  49.4 10.9 fusion.37
  60.9 66.1 %all-reduce.4 = (f32[32,32]{0,1:T(8,128)S(1)}, f32[32,32]{0,1:T(8,128)S(1)}) all-reduce(f32[32,32]{0,1:T(8,128)S(1)} %fusion.38, f32[32,32]{0,1:T(8,128)S(1)} %convolution_bitcast_fusion.3), channel_id=1, replica_groups=mesh['grp'=4,'st'=32] {'grp','st'}, use_global_device_ids=true, to_apply=%region_2.2 | all-reduce | flops 2048 | bytes 16384 | tf_op jit(solution)/shard_map/while/body/eval_jaxpr/psum | solution.py:59
  171.5 10.9 fusion.37
  182.9 64.7 %all-reduce.4 = (f32[32,32]{0,1:T(8,128)S(1)}, f32[32,32]{0,1:T(8,128)S(1)}) all-reduce(f32[32,32]{0,1:T(8,128)S(1)} %fusion.38, f32[32,32]{0,1:T(8,128)S(1)} %convolution_bitcast_fusion.3), channel_id=1, replica_groups=mesh['grp'=4,'st'=32] {'grp','st'}, use_global_device_ids=true, to_apply=%region_2.2 | all-reduce | flops 2048 | bytes 16384 | tf_op jit(solution)/shard_map/while/body/eval_jaxpr/psum | solution.py:59
  292.6 10.9 fusion.37
  304.1 64.7 %all-reduce.4 = (f32[32,32]{0,1:T(8,128)S(1)}, f32[32,32]{0,1:T(8,128)S(1)}) all-reduce(f32[32,32]{0,1:T(8,128)S(1)} %fusion.38, f32[32,32]{0,1:T(8,128)S(1)} %convolution_bitcast_fusion.3), channel_id=1, replica_groups=mesh['grp'=4,'st'=32] {'grp','st'}, use_global_device_ids=true, to_apply=%region_2.2 | all-reduce | flops 2048 | bytes 16384 | tf_op jit(solution)/shard_map/while/body/eval_jaxpr/psum | solution.py:59
  413.6 10.9 fusion.37
  425.0 64.6 %all-reduce.4 = (f32[32,32]{0,1:T(8,128)S(1)}, f32[32,32]{0,1:T(8,128)S(1)}) all-reduce(f32[32,32]{0,1:T(8,128)S(1)} %fusion.38, f32[32,32]{0,1:T(8,128)S(1)} %convolution_bitcast_fusion.3), channel_id=1, replica_groups=mesh['grp'=4,'st'=32] {'grp','st'}, use_global_device_ids=true, to_apply=%region_2.2 | all-reduce | flops 2048 | bytes 16384 | tf_op jit(solution)/shard_map/while/body/eval_jaxpr/psum | solution.py:59
  534.7 10.9 fusion.37
  546.1 64.7 %all-reduce.4 = (f32[32,32]{0,1:T(8,128)S(1)}, f32[32,32]{0,1:T(8,128)S(1)}) all-reduce(f32[32,32]{0,1:T(8,128)S(1)} %fusion.38, f32[32,32]{0,1:T(8,128)S(1)} %convolution_bitcast_fusion.3), channel_id=1, replica_groups=mesh['grp'=4,'st'=32] {'grp','st'}, use_global_device_ids=true, to_apply=%region_2.2 | all-reduce | flops 2048 | bytes 16384 | tf_op jit(solution)/shard_map/while/body/eval_jaxpr/psum | solution.py:59
  655.6 10.9 fusion.37
  667.1 64.6 %all-reduce.4 = (f32[32,32]{0,1:T(8,128)S(1)}, f32[32,32]{0,1:T(8,128)S(1)}) all-reduce(f32[32,32]{0,1:T(8,128)S(1)} %fusion.38, f32[32,32]{0,1:T(8,128)S(1)} %convolution_bitcast_fusion.3), channel_id=1, replica_groups=mesh['grp'=4,'st'=32] {'grp','st'}, use_global_device_ids=true, to_apply=%region_2.2 | all-reduce | flops 2048 | bytes 16384 | tf_op jit(solution)/shard_map/while/body/eval_jaxpr/psum | solution.py:59
  776.7 10.9 fusion.37
  788.1 64.7 %all-reduce.4 = (f32[32,32]{0,1:T(8,128)S(1)}, f32[32,32]{0,1:T(8,128)S(1)}) all-reduce(f32[32,32]{0,1:T(8,128)S(1)} %fusion.38, f32[32,32]{0,1:T(8,128)S(1)} %convolution_bitcast_fusion.3), channel_id=1, replica_groups=mesh['grp'=4,'st'=32] {'grp','st'}, use_global_device_ids=true, to_apply=%region_2.2 | all-reduce | flops 2048 | bytes 16384 | tf_op jit(solution)/shard_map/while/body/eval_jaxpr/psum | solution.py:59
  897.7 10.9 fusion.37
  909.1 64.6 %all-reduce.4 = (f32[32,32]{0,1:T(8,128)S(1)}, f32[32,32]{0,1:T(8,128)S(1)}) all-reduce(f32[32,32]{0,1:T(8,128)S(1)} %fusion.38, f32[32,32]{0,1:T(8,128)S(1)} %convolution_bitcast_fusion.3), channel_id=1, replica_groups=mesh['grp'=4,'st'=32] {'grp','st'}, use_global_device_ids=true, to_apply=%region_2.2 | all-reduce | flops 2048 | bytes 16384 | tf_op jit(solution)/shard_map/while/body/eval_jaxpr/psum | solution.py:59
  1030.1 64.7 %all-reduce.4 = (f32[32,32]{0,1:T(8,128)S(1)}, f32[32,32]{0,1:T(8,128)S(1)}) all-reduce(f32[32,32]{0,1:T(8,128)S(1)} %fusion.38, f32[32,32]{0,1:T(8,128)S(1)} %convolution_bitcast_fusion.3), channel_id=1, replica_groups=mesh['grp'=4,'st'=32] {'grp','st'}, use_global_device_ids=true, to_apply=%region_2.2 | all-reduce | flops 2048 | bytes 16384 | tf_op jit(solution)/shard_map/while/body/eval_jaxpr/psum | solution.py:59
  1139.7 10.9 fusion.37
  1151.1 64.6 %all-reduce.4 = (f32[32,32]{0,1:T(8,128)S(1)}, f32[32,32]{0,1:T(8,128)S(1)}) all-reduce(f32[32,32]{0,1:T(8,128)S(1)} %fusion.38, f32[32,32]{0,1:T(8,128)S(1)} %convolution_bitcast_fusion.3), channel_id=1, replica_groups=mesh['grp'=4,'st'=32] {'grp','st'}, use_global_device_ids=true, to_apply=%region_2.2 | all-reduce | flops 2048 | bytes 16384 | tf_op jit(solution)/shard_map/while/body/eval_jaxpr/psum | solution.py:59
  1260.7 10.9 fusion.37
  1272.1 64.7 %all-reduce.4 = (f32[32,32]{0,1:T(8,128)S(1)}, f32[32,32]{0,1:T(8,128)S(1)}) all-reduce(f32[32,32]{0,1:T(8,128)S(1)} %fusion.38, f32[32,32]{0,1:T(8,128)S(1)} %convolution_bitcast_fusion.3), channel_id=1, replica_groups=mesh['grp'=4,'st'=32] {'grp','st'}, use_global_device_ids=true, to_apply=%region_2.2 | all-reduce | flops 2048 | bytes 16384 | tf_op jit(solution)/shard_map/while/body/eval_jaxpr/psum | solution.py:59
  1381.7 10.9 fusion.37
  1393.1 64.6 %all-reduce.4 = (f32[32,32]{0,1:T(8,128)S(1)}, f32[32,32]{0,1:T(8,128)S(1)}) all-reduce(f32[32,32]{0,1:T(8,128)S(1)} %fusion.38, f32[32,32]{0,1:T(8,128)S(1)} %convolution_bitcast_fusion.3), channel_id=1, replica_groups=mesh['grp'=4,'st'=32] {'grp','st'}, use_global_device_ids=true, to_apply=%region_2.2 | all-reduce | flops 2048 | bytes 16384 | tf_op jit(solution)/shard_map/while/body/eval_jaxpr/psum | solution.py:59
  (687 shorter events, 634.2 us)
Async XLA Ops:
  9.7 22.1 %collective-permute-start = (bf16[32,1024]{1,0:T(8,128)(2,1)S(1)}, bf16[32,1024]{1,0:T(8,128)(2,1)S(1)}, u32[]{:S(2)}, u32[]{:S(2)}) collective-permute-start(bf16[32,1024]{1,0:T(8,128)(2,1)S(1)} %convert_element_type.15), channel_id=1, source_target_pairs={{0,4},{1,5},{2,6},{3,7},{4,8},{5,9},{6,10},{7,11},{8,12},{9,13},{1... | collective-permute-start | bytes 196616 | tf_op jit(solution)/shard_map/while/body/eval_jaxpr/ppermute | solution.py:12
  13.7 20.5 %collective-permute-start.1 = (bf16[32,1024]{1,0:T(8,128)(2,1)S(1)}, bf16[32,1024]{1,0:T(8,128)(2,1)S(1)}, u32[]{:S(2)}, u32[]{:S(2)}) collective-permute-start(bf16[32,1024]{1,0:T(8,128)(2,1)S(1)} %convert_element_type.15), channel_id=1, source_target_pairs={{0,3},{1,4},{2,5},{3,6},{4,7},{5,8},{6,9},{7,10},{8,11},{9,12},{10... | collective-permute-start | bytes 196616 | tf_op jit(solution)/shard_map/while/body/eval_jaxpr/ppermute | solution.py:12
  21.8 20.6 %collective-permute-start.3 = (bf16[32,1024]{1,0:T(8,128)(2,1)S(1)}, bf16[32,1024]{1,0:T(8,128)(2,1)S(1)}, u32[]{:S(2)}, u32[]{:S(2)}) collective-permute-start(bf16[32,1024]{1,0:T(8,128)(2,1)S(1)} %convert_element_type.15), channel_id=1, source_target_pairs={{0,1},{1,2},{2,3},{3,4},{4,5},{5,6},{6,7},{7,8},{8,9},{9,10},{10,1... | collective-permute-start | bytes 196616 | tf_op jit(solution)/shard_map/while/body/eval_jaxpr/ppermute | solution.py:12
  144.0 20.4 %collective-permute-start.3 = (bf16[32,1024]{1,0:T(8,128)(2,1)S(1)}, bf16[32,1024]{1,0:T(8,128)(2,1)S(1)}, u32[]{:S(2)}, u32[]{:S(2)}) collective-permute-start(bf16[32,1024]{1,0:T(8,128)(2,1)S(1)} %convert_element_type.15), channel_id=1, source_target_pairs={{0,1},{1,2},{2,3},{3,4},{4,5},{5,6},{6,7},{7,8},{8,9},{9,10},{10,1... | collective-permute-start | bytes 196616 | tf_op jit(solution)/shard_map/while/body/eval_jaxpr/ppermute | solution.py:12
  260.9 20.5 %collective-permute-start.2 = (bf16[32,1024]{1,0:T(8,128)(2,1)S(1)}, bf16[32,1024]{1,0:T(8,128)(2,1)S(1)}, u32[]{:S(2)}, u32[]{:S(2)}) collective-permute-start(bf16[32,1024]{1,0:T(8,128)(2,1)S(1)} %convert_element_type.15), channel_id=1, source_target_pairs={{0,2},{1,3},{2,4},{3,5},{4,6},{5,7},{6,8},{7,9},{8,10},{9,11},{10,... | collective-permute-start | bytes 196616 | tf_op jit(solution)/shard_map/while/body/eval_jaxpr/ppermute | solution.py:12
  264.7 20.9 %collective-permute-start.3 = (bf16[32,1024]{1,0:T(8,128)(2,1)S(1)}, bf16[32,1024]{1,0:T(8,128)(2,1)S(1)}, u32[]{:S(2)}, u32[]{:S(2)}) collective-permute-start(bf16[32,1024]{1,0:T(8,128)(2,1)S(1)} %convert_element_type.15), channel_id=1, source_target_pairs={{0,1},{1,2},{2,3},{3,4},{4,5},{5,6},{6,7},{7,8},{8,9},{9,10},{10,1... | collective-permute-start | bytes 196616 | tf_op jit(solution)/shard_map/while/body/eval_jaxpr/ppermute | solution.py:12
  382.4 20.5 %collective-permute-start.2 = (bf16[32,1024]{1,0:T(8,128)(2,1)S(1)}, bf16[32,1024]{1,0:T(8,128)(2,1)S(1)}, u32[]{:S(2)}, u32[]{:S(2)}) collective-permute-start(bf16[32,1024]{1,0:T(8,128)(2,1)S(1)} %convert_element_type.15), channel_id=1, source_target_pairs={{0,2},{1,3},{2,4},{3,5},{4,6},{5,7},{6,8},{7,9},{8,10},{9,11},{10,... | collective-permute-start | bytes 196616 | tf_op jit(solution)/shard_map/while/body/eval_jaxpr/ppermute | solution.py:12
  385.9 20.5 %collective-permute-start.3 = (bf16[32,1024]{1,0:T(8,128)(2,1)S(1)}, bf16[32,1024]{1,0:T(8,128)(2,1)S(1)}, u32[]{:S(2)}, u32[]{:S(2)}) collective-permute-start(bf16[32,1024]{1,0:T(8,128)(2,1)S(1)} %convert_element_type.15), channel_id=1, source_target_pairs={{0,1},{1,2},{2,3},{3,4},{4,5},{5,6},{6,7},{7,8},{8,9},{9,10},{10,1... | collective-permute-start | bytes 196616 | tf_op jit(solution)/shard_map/while/body/eval_jaxpr/ppermute | solution.py:12
  503.2 20.5 %collective-permute-start.2 = (bf16[32,1024]{1,0:T(8,128)(2,1)S(1)}, bf16[32,1024]{1,0:T(8,128)(2,1)S(1)}, u32[]{:S(2)}, u32[]{:S(2)}) collective-permute-start(bf16[32,1024]{1,0:T(8,128)(2,1)S(1)} %convert_element_type.15), channel_id=1, source_target_pairs={{0,2},{1,3},{2,4},{3,5},{4,6},{5,7},{6,8},{7,9},{8,10},{9,11},{10,... | collective-permute-start | bytes 196616 | tf_op jit(solution)/shard_map/while/body/eval_jaxpr/ppermute | solution.py:12
  506.7 20.9 %collective-permute-start.3 = (bf16[32,1024]{1,0:T(8,128)(2,1)S(1)}, bf16[32,1024]{1,0:T(8,128)(2,1)S(1)}, u32[]{:S(2)}, u32[]{:S(2)}) collective-permute-start(bf16[32,1024]{1,0:T(8,128)(2,1)S(1)} %convert_element_type.15), channel_id=1, source_target_pairs={{0,1},{1,2},{2,3},{3,4},{4,5},{5,6},{6,7},{7,8},{8,9},{9,10},{10,1... | collective-permute-start | bytes 196616 | tf_op jit(solution)/shard_map/while/body/eval_jaxpr/ppermute | solution.py:12
  624.4 20.5 %collective-permute-start.2 = (bf16[32,1024]{1,0:T(8,128)(2,1)S(1)}, bf16[32,1024]{1,0:T(8,128)(2,1)S(1)}, u32[]{:S(2)}, u32[]{:S(2)}) collective-permute-start(bf16[32,1024]{1,0:T(8,128)(2,1)S(1)} %convert_element_type.15), channel_id=1, source_target_pairs={{0,2},{1,3},{2,4},{3,5},{4,6},{5,7},{6,8},{7,9},{8,10},{9,11},{10,... | collective-permute-start | bytes 196616 | tf_op jit(solution)/shard_map/while/body/eval_jaxpr/ppermute | solution.py:12
  627.9 20.5 %collective-permute-start.3 = (bf16[32,1024]{1,0:T(8,128)(2,1)S(1)}, bf16[32,1024]{1,0:T(8,128)(2,1)S(1)}, u32[]{:S(2)}, u32[]{:S(2)}) collective-permute-start(bf16[32,1024]{1,0:T(8,128)(2,1)S(1)} %convert_element_type.15), channel_id=1, source_target_pairs={{0,1},{1,2},{2,3},{3,4},{4,5},{5,6},{6,7},{7,8},{8,9},{9,10},{10,1... | collective-permute-start | bytes 196616 | tf_op jit(solution)/shard_map/while/body/eval_jaxpr/ppermute | solution.py:12
  745.2 20.5 %collective-permute-start.2 = (bf16[32,1024]{1,0:T(8,128)(2,1)S(1)}, bf16[32,1024]{1,0:T(8,128)(2,1)S(1)}, u32[]{:S(2)}, u32[]{:S(2)}) collective-permute-start(bf16[32,1024]{1,0:T(8,128)(2,1)S(1)} %convert_element_type.15), channel_id=1, source_target_pairs={{0,2},{1,3},{2,4},{3,5},{4,6},{5,7},{6,8},{7,9},{8,10},{9,11},{10,... | collective-permute-start | bytes 196616 | tf_op jit(solution)/shard_map/while/body/eval_jaxpr/ppermute | solution.py:12
  748.8 20.8 %collective-permute-start.3 = (bf16[32,1024]{1,0:T(8,128)(2,1)S(1)}, bf16[32,1024]{1,0:T(8,128)(2,1)S(1)}, u32[]{:S(2)}, u32[]{:S(2)}) collective-permute-start(bf16[32,1024]{1,0:T(8,128)(2,1)S(1)} %convert_element_type.15), channel_id=1, source_target_pairs={{0,1},{1,2},{2,3},{3,4},{4,5},{5,6},{6,7},{7,8},{8,9},{9,10},{10,1... | collective-permute-start | bytes 196616 | tf_op jit(solution)/shard_map/while/body/eval_jaxpr/ppermute | solution.py:12
  866.4 20.5 %collective-permute-start.2 = (bf16[32,1024]{1,0:T(8,128)(2,1)S(1)}, bf16[32,1024]{1,0:T(8,128)(2,1)S(1)}, u32[]{:S(2)}, u32[]{:S(2)}) collective-permute-start(bf16[32,1024]{1,0:T(8,128)(2,1)S(1)} %convert_element_type.15), channel_id=1, source_target_pairs={{0,2},{1,3},{2,4},{3,5},{4,6},{5,7},{6,8},{7,9},{8,10},{9,11},{10,... | collective-permute-start | bytes 196616 | tf_op jit(solution)/shard_map/while/body/eval_jaxpr/ppermute | solution.py:12
  870.0 20.5 %collective-permute-start.3 = (bf16[32,1024]{1,0:T(8,128)(2,1)S(1)}, bf16[32,1024]{1,0:T(8,128)(2,1)S(1)}, u32[]{:S(2)}, u32[]{:S(2)}) collective-permute-start(bf16[32,1024]{1,0:T(8,128)(2,1)S(1)} %convert_element_type.15), channel_id=1, source_target_pairs={{0,1},{1,2},{2,3},{3,4},{4,5},{5,6},{6,7},{7,8},{8,9},{9,10},{10,1... | collective-permute-start | bytes 196616 | tf_op jit(solution)/shard_map/while/body/eval_jaxpr/ppermute | solution.py:12
  987.2 20.5 %collective-permute-start.2 = (bf16[32,1024]{1,0:T(8,128)(2,1)S(1)}, bf16[32,1024]{1,0:T(8,128)(2,1)S(1)}, u32[]{:S(2)}, u32[]{:S(2)}) collective-permute-start(bf16[32,1024]{1,0:T(8,128)(2,1)S(1)} %convert_element_type.15), channel_id=1, source_target_pairs={{0,2},{1,3},{2,4},{3,5},{4,6},{5,7},{6,8},{7,9},{8,10},{9,11},{10,... | collective-permute-start | bytes 196616 | tf_op jit(solution)/shard_map/while/body/eval_jaxpr/ppermute | solution.py:12
  990.8 20.8 %collective-permute-start.3 = (bf16[32,1024]{1,0:T(8,128)(2,1)S(1)}, bf16[32,1024]{1,0:T(8,128)(2,1)S(1)}, u32[]{:S(2)}, u32[]{:S(2)}) collective-permute-start(bf16[32,1024]{1,0:T(8,128)(2,1)S(1)} %convert_element_type.15), channel_id=1, source_target_pairs={{0,1},{1,2},{2,3},{3,4},{4,5},{5,6},{6,7},{7,8},{8,9},{9,10},{10,1... | collective-permute-start | bytes 196616 | tf_op jit(solution)/shard_map/while/body/eval_jaxpr/ppermute | solution.py:12
  1108.4 20.5 %collective-permute-start.2 = (bf16[32,1024]{1,0:T(8,128)(2,1)S(1)}, bf16[32,1024]{1,0:T(8,128)(2,1)S(1)}, u32[]{:S(2)}, u32[]{:S(2)}) collective-permute-start(bf16[32,1024]{1,0:T(8,128)(2,1)S(1)} %convert_element_type.15), channel_id=1, source_target_pairs={{0,2},{1,3},{2,4},{3,5},{4,6},{5,7},{6,8},{7,9},{8,10},{9,11},{10,... | collective-permute-start | bytes 196616 | tf_op jit(solution)/shard_map/while/body/eval_jaxpr/ppermute | solution.py:12
  1112.0 20.5 %collective-permute-start.3 = (bf16[32,1024]{1,0:T(8,128)(2,1)S(1)}, bf16[32,1024]{1,0:T(8,128)(2,1)S(1)}, u32[]{:S(2)}, u32[]{:S(2)}) collective-permute-start(bf16[32,1024]{1,0:T(8,128)(2,1)S(1)} %convert_element_type.15), channel_id=1, source_target_pairs={{0,1},{1,2},{2,3},{3,4},{4,5},{5,6},{6,7},{7,8},{8,9},{9,10},{10,1... | collective-permute-start | bytes 196616 | tf_op jit(solution)/shard_map/while/body/eval_jaxpr/ppermute | solution.py:12
  1229.3 20.5 %collective-permute-start.2 = (bf16[32,1024]{1,0:T(8,128)(2,1)S(1)}, bf16[32,1024]{1,0:T(8,128)(2,1)S(1)}, u32[]{:S(2)}, u32[]{:S(2)}) collective-permute-start(bf16[32,1024]{1,0:T(8,128)(2,1)S(1)} %convert_element_type.15), channel_id=1, source_target_pairs={{0,2},{1,3},{2,4},{3,5},{4,6},{5,7},{6,8},{7,9},{8,10},{9,11},{10,... | collective-permute-start | bytes 196616 | tf_op jit(solution)/shard_map/while/body/eval_jaxpr/ppermute | solution.py:12
  1232.8 20.8 %collective-permute-start.3 = (bf16[32,1024]{1,0:T(8,128)(2,1)S(1)}, bf16[32,1024]{1,0:T(8,128)(2,1)S(1)}, u32[]{:S(2)}, u32[]{:S(2)}) collective-permute-start(bf16[32,1024]{1,0:T(8,128)(2,1)S(1)} %convert_element_type.15), channel_id=1, source_target_pairs={{0,1},{1,2},{2,3},{3,4},{4,5},{5,6},{6,7},{7,8},{8,9},{9,10},{10,1... | collective-permute-start | bytes 196616 | tf_op jit(solution)/shard_map/while/body/eval_jaxpr/ppermute | solution.py:12
  1350.4 20.5 %collective-permute-start.2 = (bf16[32,1024]{1,0:T(8,128)(2,1)S(1)}, bf16[32,1024]{1,0:T(8,128)(2,1)S(1)}, u32[]{:S(2)}, u32[]{:S(2)}) collective-permute-start(bf16[32,1024]{1,0:T(8,128)(2,1)S(1)} %convert_element_type.15), channel_id=1, source_target_pairs={{0,2},{1,3},{2,4},{3,5},{4,6},{5,7},{6,8},{7,9},{8,10},{9,11},{10,... | collective-permute-start | bytes 196616 | tf_op jit(solution)/shard_map/while/body/eval_jaxpr/ppermute | solution.py:12
  1354.0 20.5 %collective-permute-start.3 = (bf16[32,1024]{1,0:T(8,128)(2,1)S(1)}, bf16[32,1024]{1,0:T(8,128)(2,1)S(1)}, u32[]{:S(2)}, u32[]{:S(2)}) collective-permute-start(bf16[32,1024]{1,0:T(8,128)(2,1)S(1)} %convert_element_type.15), channel_id=1, source_target_pairs={{0,1},{1,2},{2,3},{3,4},{4,5},{5,6},{6,7},{7,8},{8,9},{9,10},{10,1... | collective-permute-start | bytes 196616 | tf_op jit(solution)/shard_map/while/body/eval_jaxpr/ppermute | solution.py:12
  (76 other events, 993.9 us)
where the time goes:
time: 1470 us
  blocking collectives  777 us (53%)
  starting transfers between devices  359 us (24%)
  matrix products  141 us (10%)
  other arithmetic  98 us (7%)
  local copies, waits for them, and re-layouts  71.8 us (5%)
  waiting for transfers between devices  15 us (1%)
    psum x12, blocking collectives, one_step(): lax.psum((gram_local, cross_local), ('grp', 'st'))  777 us
    ppermute x96, starting transfers between devices, shifted(): return lax.ppermute(shard, axis, pairs)  359 us
    dot_general x12, matrix products, band_terms(): jnp.einsum('nkw,nrw->nkr', windows, shaped, preferred_element_type=jnp.fl...  130 us
    gather x144, local copies, waits for them, and re-layouts  68.4 us
    another operation x36, other arithmetic, one_step(): lower_factor = jnp.linalg.cholesky(gram_matrix)  43.1 us
    another operation x24, other arithmetic, one_step(): lax.linalg.triangular_solve(lower_factor, image, left_side=True, lower=True)  37 us
  transfers between devices with their start and end apart: 96, of which 12 were waited for; matrix products, arithmetic and copies ran while one was open for 0% of the time, Pallas kernels for 0%

commit v1 on v0

v1 whole, which is shorter than its diff:
```python
import functools

import jax
import jax.numpy as jnp
from jax import lax
from jax.experimental import pallas as pl
from jax.experimental.pallas import tpu as pltpu
from jax.sharding import PartitionSpec as P

ITERS = 12
MESH = pl.DeviceIdType.MESH
F32 = jnp.float32
BF16 = jnp.bfloat16
LANE = 128
SIZES = {"yh": 2, "core": 2, "z": 4, "yl": 2, "x": 4}
PHASES = (("yh", "yl", "x"), ("core", "z"))


def split3(value):
    high = value.astype(BF16)
    rest = value - high.astype(F32)
    mid = rest.astype(BF16)
    low = (rest - mid.astype(F32)).astype(BF16)
    return high, mid, low


def coordinates():
    grp, st = lax.axis_index("grp"), lax.axis_index("st")
    return {"yh": grp // 2, "core": grp % 2, "z": st // 8, "yl": (st // 4) % 2, "x": st % 4}


def device_of(at):
    return (at["yh"] * 2 + at["core"], at["z"] * 8 + at["yl"] * 4 + at["x"])


def group(at, names):
    place = 0
    for name in names:
        place = place * SIZES[name] + at[name]
    count = 1
    for name in names:
        count *= SIZES[name]
    others = []
    for code in range(1, count):
        peer, rest = dict(at), code
        for name in reversed(names):
            step = rest % SIZES[name]
            rest //= SIZES[name]
            if step:
                peer[name] = (at[name] + step) % SIZES[name]
        others.append(device_of(peer))
    return place, count, others


def tree_sum(items):
    items = list(items)
    while len(items) > 1:
        items = [a + b for a, b in zip(items[::2], items[1::2])] + ([items[-1]] if len(items) % 2 else [])
    return items[0]


def inverse_factor(gram_rows):
    shape = (8, LANE)
    row8 = lax.broadcasted_iota(jnp.int32, shape, 0)
    lane = lax.broadcasted_iota(jnp.int32, shape, 1)
    g = list(gram_rows)
    inv = [jnp.where(lane % 32 == row8 + 8 * q, F32(1), F32(0)) for q in range(4)]
    out = []
    for p in range(4):
        cols = [[jnp.broadcast_to(g[q][:, 8 * p + k : 8 * p + k + 1], shape) for q in range(p, 4)] for k in range(8)]
        diag = jnp.ones(shape, F32)
        for j in range(8):
            pivot = jnp.broadcast_to(cols[j][0][j : j + 1, :], shape)
            diag = jnp.where(row8 == j, pivot, diag)
            scale = 1.0 / pivot
            factors = [col * scale for col in cols[j]]
            factors[0] = jnp.where(row8 > j, factors[0], F32(0))
            for k in range(j + 1, 8):
                head = jnp.broadcast_to(cols[k][0][j : j + 1, :], shape)
                cols[k] = [col - factor * head for col, factor in zip(cols[k], factors)]
            row_g = jnp.broadcast_to(g[p][j : j + 1, :], shape)
            row_i = jnp.broadcast_to(inv[p][j : j + 1, :], shape)
            for q in range(p, 4):
                if q == p and j == 7:
                    continue
                if q > p or p < 3:
                    g[q] = g[q] - factors[q - p] * row_g
                inv[q] = inv[q] - factors[q - p] * row_i
        out.append(inv[p] * (1.0 / jnp.sqrt(diag)))
    return jnp.concatenate(out, axis=0)


def align(first_ref, width_ref, band_ref, weights, raw, sem):
    blocks, block_rows = raw.shape[0], raw.shape[1]
    window = weights.shape[0]
    loads = []
    for b in range(blocks):
        load = pltpu.make_async_copy(band_ref.at[pl.ds(b * block_rows, block_rows), :], raw.at[b], sem.at[b])
        load.start()
        loads.append(load)
    for b in range(blocks):
        here = slice(b * block_rows, (b + 1) * block_rows)
        loads[b].wait()
        first = first_ref[b] // LANE
        used = width_ref[b] // LANE

        def clear(e, carry, here=here):
            weights[pl.ds(pl.multiple_of(e * LANE, LANE), LANE), here] = jnp.zeros((LANE, block_rows), BF16)
            return carry

        def turn(e, carry, b=b, here=here, first=first):
            piece = raw[b, :, pl.ds(pl.multiple_of(e * LANE, LANE), LANE)]
            weights[pl.ds(pl.multiple_of((first + e) * LANE, LANE), LANE), here] = jnp.transpose(piece)
            return carry

        lax.fori_loop(0, first, clear, 0)
        lax.fori_loop(first + used, window // LANE, clear, 0)
        lax.fori_loop(0, used, turn, 0)


def kernel(
    start_ref, stay_ref, weights,
    out_ref, ritz_ref,
    xbuf, current, image, scale, acc,
    gram1, gram2, cross1, cross2,
    halo_send, halo_recv, send1, recv1, send2, recv2, csend, crecv,
):
    count, rows = start_ref.shape
    reach = (xbuf.shape[0] - 1) // 2
    devices = lax.axis_size("grp") * lax.axis_size("st")
    members = lax.axis_size("st")
    chain = lax.axis_index("grp") * members + lax.axis_index("st")
    at = coordinates()
    place1, count1, others1 = group(at, PHASES[0])
    place2, count2, others2 = group(at, PHASES[1])

    x = at["x"]

    def chained(by):
        there = lax.rem(chain + by + devices, devices)
        return (there // members, there % members)

    right = device_of({**at, "x": (x + 1) % 4})
    left = device_of({**at, "x": (x + 3) % 4})
    following, preceding = chained(4), chained(-4)
    neighbours = (right, left, following, preceding)

    barrier = pltpu.get_barrier_semaphore()
    for device in neighbours:
        pl.semaphore_signal(barrier, inc=1, device_id=device, device_id_type=MESH)
    for device in others1 + others2:
        pl.semaphore_signal(barrier, inc=1, device_id=device, device_id_type=MESH)

    current[...] = start_ref[...]
    xbuf[reach] = start_ref[...].astype(BF16)

    def pick(condition, first, second):
        return jnp.where(condition, reach + first, reach + second)

    def sending(which, arriving, src, dst, device):
        return pltpu.make_async_remote_copy(
            src_ref=src,
            dst_ref=dst,
            send_sem=halo_send.at[which],
            recv_sem=halo_recv.at[arriving],
            device_id=device,
            device_id_type=MESH,
        )

    def block_to(which, arriving, src, dst, device):
        return sending(which, arriving, xbuf.at[src], xbuf.at[dst], device)

    from_left, from_right = pick(x == 0, 3, -1), pick(x < 3, 1, -3)
    across = pick(x < 2, 2, -2)
    row_left, row_right = pick(x == 0, -1, 3), pick(x == 3, 1, -3)
    row_across = pick(x < 2, -2, 2)
    middle = jnp.logical_and(x >= 1, x <= 2)
    own = [
        block_to(2, 2, reach, reach - 4, following),
        block_to(3, 3, reach, reach + 4, preceding),
        block_to(0, 0, reach, pick(x == 3, 3, -1), right),
        block_to(1, 1, reach, pick(x >= 1, 1, -3), left),
    ]
    half = count // 2
    halves = []
    for which, src, first, dst, device in (
        (4, from_left, 0, pick(jnp.logical_or(x == 3, x == 0), 2, -2), right),
        (5, from_right, half, pick(middle, 2, -2), left),
    ):
        rows_of = pl.ds(first, half)
        halves.append(sending(which, which, xbuf.at[src, rows_of], xbuf.at[dst, rows_of], device))
    along = [
        block_to(6, 6, pick(x == 3, -4, 4), pick(x == 3, -1, 3), right),
        block_to(7, 7, pick(x >= 1, -4, 4), pick(x >= 1, -3, 1), left),
    ]
    onward = [
        block_to(8, 8, reach + 3, reach + 2, right),
        block_to(9, 8, reach - 3, reach - 2, left),
    ]

    def arrived(which, slot, rows_of=None):
        part = xbuf.at[slot] if rows_of is None else xbuf.at[slot, rows_of]
        pltpu.make_async_copy(part, part, halo_recv.at[which]).wait()

    pl.semaphore_wait(barrier, len(neighbours) + len(others1) + len(others2))
    for copy in own:
        copy.start()

    def stored(slot):
        return weights[pl.ds(pl.multiple_of(slot * rows, rows), rows), :]

    def product(slot):
        there = chain + (slot - reach)
        valid = jnp.where(jnp.logical_and(there >= 0, there < devices), F32(1), F32(0)).astype(BF16)
        return jnp.dot(xbuf[slot] * valid, stored(slot), preferred_element_type=F32)

    ones = jnp.ones((16, rows), BF16)
    sums = lax.fori_loop(
        0,
        2 * reach + 1,
        lambda slot, total: total + jnp.dot(ones, stored(slot), preferred_element_type=F32)[0:8],
        jnp.zeros((8, rows), F32),
    )
    scale[...] = (1.0 - stay_ref[...]) / sums[0:1]

    lane8 = lax.broadcasted_iota(jnp.int32, (8, LANE), 1) // 32
    lane32 = lax.broadcasted_iota(jnp.int32, (count, LANE), 1) // 32

    def packed_product(left3, right3):
        left = jnp.concatenate(left3, axis=0)
        right = jnp.concatenate([piece for piece in right3 for _ in range(4)], axis=0)
        terms = lax.dot_general(left, right, (((1,), (1,)), ((), ())), preferred_element_type=F32)
        full = tree_sum(terms[32 * a : 32 * a + 32, LANE * b : LANE * b + LANE] for a in (2, 1, 0) for b in (2, 1, 0))
        tile = full[0:8]
        for q in range(1, 4):
            tile = jnp.where(lane8 == q, full[8 * q : 8 * q + 8], tile)
        return tile * (1.0 / (rows * devices))

    def unpacked(tile):
        return [tile] + [pltpu.roll(tile, LANE - 32 * q, 1) for q in range(1, 4)]

    def send_all(buffer, place, others, send_sem, recv_sem):
        for device in others:
            pltpu.make_async_remote_copy(
                src_ref=buffer.at[place],
                dst_ref=buffer.at[place],
                send_sem=send_sem,
                recv_sem=recv_sem,
                device_id=device,
                device_id_type=MESH,
            ).start()

    def wait_all(buffer, others, sem):
        part = buffer.at[pl.ds(0, len(others))]
        pltpu.make_async_copy(part, part, sem).wait()

    def summed(buffer, n):
        return tree_sum(buffer[i] for i in range(n))

    def one_step(t, carry):
        parity = t % 2
        final = t == ITERS - 1
        acc[...] = product(reach)
        arrived(0, from_left)
        halves[0].start()
        arrived(1, from_right)
        halves[1].start()
        acc[...] += product(from_left) + product(from_right)
        arrived(2, reach - 4)
        arrived(3, reach + 4)
        for copy in along:
            copy.start()
        acc[...] += product(reach - 4) + product(reach + 4)
        arrived(4, across, pl.ds(0, half))
        arrived(5, across, pl.ds(half, half))
        acc[...] += product(across)
        arrived(6, row_left)
        arrived(7, row_right)

        @pl.when(middle)
        def _():
            for copy in onward:
                copy.start()

        acc[...] += product(row_left) + product(row_right)
        arrived(8, row_across)
        acc[...] += product(row_across)
        for copy in halves + along:
            copy.wait_send()

        @pl.when(middle)
        def _():
            for copy in onward:
                copy.wait_send()

        image[...] = stay_ref[...] * current[...] + scale[...] * acc[...]
        pieces = split3(image[...])
        buf1, buf2 = gram1.at[parity], gram2.at[parity]
        buf1[place1] = packed_product(pieces, pieces)
        send_all(buf1, place1, others1, send1, recv1.at[parity])

        @pl.when(final)
        def _():
            cross1[place1] = packed_product(split3(current[...]), pieces)
            send_all(cross1, place1, others1, csend.at[0], crecv.at[0])

        wait_all(buf1, others1, recv1.at[parity])
        buf2[place2] = summed(buf1, count1)
        send_all(buf2, place2, others2, send2, recv2.at[parity])

        @pl.when(final)
        def _():
            wait_all(cross1, others1, crecv.at[0])
            cross2[place2] = summed(cross1, count1)
            send_all(cross2, place2, others2, csend.at[1], crecv.at[1])

        wait_all(buf2, others2, recv2.at[parity])
        gram = unpacked(summed(buf2, count2))
        wait_all(buf1, others1, send1)
        wait_all(buf2, others2, send2)

        inverse = inverse_factor(gram)
        high, mid, low = (piece.astype(F32) for piece in split3(inverse))
        left_a = jnp.where(lane32 < 2, high, mid)
        left_b = jnp.where(lane32 == 0, high, jnp.where(lane32 == 2, mid, low))
        left = jnp.concatenate([left_a, left_b], axis=1).astype(BF16)
        ih, im, il = pieces
        right = jnp.concatenate([ih, im, ih, im, il, ih, il, im], axis=0)
        updated = jnp.dot(left, right, preferred_element_type=F32)
        current[...] = updated
        for copy in own:
            copy.wait_send()
        xbuf[reach] = updated.astype(BF16)

        @pl.when(jnp.logical_not(final))
        def _():
            for copy in own:
                copy.start()

        return carry

    lax.fori_loop(0, ITERS, one_step, 0)

    out_ref[...] = current[...]
    wait_all(cross2, others2, crecv.at[1])
    ritz = unpacked(summed(cross2, count2))
    for q in range(4):
        ritz_ref[8 * q : 8 * q + 8, :] = ritz[q][:, 0:32]
    wait_all(cross1, others1, csend.at[0])
    wait_all(cross2, others2, csend.at[1])


def shards(start_vectors, stay, band_blocks, band_start, band_width):
    count, rows = start_vectors.shape
    span = band_blocks.shape[1]
    blocks = band_start.shape[0]
    reach = span // (2 * rows)
    window = 2 * reach + 1
    vmem = pl.BlockSpec(memory_space=pltpu.VMEM)
    smem = pl.BlockSpec(memory_space=pltpu.SMEM)
    members1 = members2 = 1
    for name in PHASES[0]:
        members1 *= SIZES[name]
    for name in PHASES[1]:
        members2 *= SIZES[name]
    stay = stay.reshape(1, rows)
    chain = lax.axis_index("grp") * lax.axis_size("st") + lax.axis_index("st")
    first = band_start - (chain - reach) * rows
    weights = pl.pallas_call(
        align,
        out_shape=pltpu.VMEM((window * rows, rows), BF16),
        in_specs=[smem, smem, pl.BlockSpec(memory_space=pl.ANY)],
        out_specs=vmem,
        scratch_shapes=[pltpu.VMEM((blocks, rows // blocks, span), BF16), pltpu.SemaphoreType.DMA((blocks,))],
        compiler_params=pltpu.CompilerParams(vmem_limit_bytes=24 * 1024 * 1024),
        name="align",
    )(first, band_width, pltpu.with_memory_space_constraint(band_blocks, pltpu.HBM))
    weights = pltpu.with_memory_space_constraint(weights, pltpu.VMEM)
    return pl.pallas_call(
        kernel,
        out_shape=(jax.ShapeDtypeStruct((count, rows), F32), jax.ShapeDtypeStruct((count, count), F32)),
        in_specs=[vmem, vmem, vmem],
        out_specs=(vmem, vmem),
        scratch_shapes=[
            pltpu.VMEM((window, count, rows), BF16),
            pltpu.VMEM((count, rows), F32),
            pltpu.VMEM((count, rows), F32),
            pltpu.VMEM((1, rows), F32),
            pltpu.VMEM((count, rows), F32),
            pltpu.VMEM((2, members1, 8, LANE), F32),
            pltpu.VMEM((2, members2, 8, LANE), F32),
            pltpu.VMEM((members1, 8, LANE), F32),
            pltpu.VMEM((members2, 8, LANE), F32),
            pltpu.SemaphoreType.DMA((10,)),
            pltpu.SemaphoreType.DMA((9,)),
            pltpu.SemaphoreType.DMA,
            pltpu.SemaphoreType.DMA((2,)),
            pltpu.SemaphoreType.DMA,
            pltpu.SemaphoreType.DMA((2,)),
            pltpu.SemaphoreType.DMA((2,)),
            pltpu.SemaphoreType.DMA((2,)),
        ],
        compiler_params=pltpu.CompilerParams(
            collective_id=0, has_side_effects=True, vmem_limit_bytes=12 * 1024 * 1024
        ),
        name="subspace",
    )(start_vectors, stay, weights)


def solution(mesh):
    placed = (
        P(None, ("grp", "st")),
        P(("grp", "st")),
        P(("grp", "st"), None),
        P(("grp", "st")),
        P(("grp", "st")),
    )
    return jax.shard_map(
        shards, mesh=mesh, in_specs=placed, out_specs=(P(None, ("grp", "st")), P()), check_vma=False
    )
```

time: 1470 us -> 298 us (0.20)
  blocking collectives: 777 us -> 0 us
  starting transfers between devices: 359 us -> 0 us
  Pallas kernels: 0 us -> 294 us
  matrix products: 141 us -> 0 us
  other arithmetic: 98 us -> 0.69 us
  local copies, waits for them, and re-layouts: 71.8 us -> 1.93 us
  waiting for transfers between devices: 15 us -> 0 us
    psum x12 -> x0, blocking collectives: 777 us -> none  [one_step(): lax.psum((gram_local, cross_local), ('grp', 'st'))]
    ppermute x96 -> x0, starting transfers between devices: 359 us -> none  [shifted(): return lax.ppermute(shard, axis, pairs)]
    pallas_call x0 -> x2, Pallas kernels: none -> 294 us  [the longest x1 275 us: shards(): pl.pallas_call(kernel, out_shape=(jax.ShapeDtypeStruct((count, rows), F32...]
    dot_general x36 -> x0, matrix products: 137 us -> none  [the longest x12 130 us: band_terms(): jnp.einsum('nkw,nrw->nkr', windows, shaped, preferred_element_type=jnp.fl...]
    another operation x60 -> x0, other arithmetic: 80.2 us -> none  [the longest x36 43.1 us: one_step(): lower_factor = jnp.linalg.cholesky(gram_matrix)]
    gather x144 -> x0, local copies, waits for them, and re-layouts: 68.4 us -> none
    ppermute x96 -> x0, waiting for transfers between devices: 15 us -> none  [shifted(): return lax.ppermute(shard, axis, pairs)]
  transfers between devices with their start and end apart: 96 -> 0, of which waited for: 12 -> 0; matrix products, arithmetic and copies ran while one was open for 0% -> 0% of each run, Pallas kernels for 0% -> 0%
where the time goes in v1:
time: 298 us; the launch traced here: 297 us
  Pallas kernels  294 us (99%)
    pallas_call x1, Pallas kernels, shards(): pl.pallas_call(kernel, out_shape=(jax.ShapeDtypeStruct((count, rows), F32...  275 us
    pallas_call x1, Pallas kernels, shards(): pl.pallas_call(align, out_shape=pltpu.VMEM((window * rows, rows), BF16),...  19 us

profile of v1, /device:TPU:1, one launch (start us, length us, event | category | flops | bytes accessed | tf_op | source)
XLA Modules:
  0.0 297.4 jit_solution(2103511066766936446)
XLA Ops:
  0.6 0.0 copy-start.1
  0.6 0.0 copy-start
  0.7 0.7 broadcast_subtract_fusion.first_ref
  1.4 0.0 copy-start.2
  1.4 0.7 copy-done.2
  2.0 19.0 %align.1.weights = bf16[9216,1024]{1,0:T(8,128)(2,1)S(1)} custom-call(s32[4]{0:T(128)S(1)} %broadcast_subtract_fusion.first_ref, s32[4]{0:T(128)S(1)} %copy-done.2, bf16[1024,8192]{1,0:T(8,128)(2,1)} %band_ref.1), custom_call_target="tpu_custom_call" | custom-call | tf_op jit(solution)/shard_map/align/pallas_call | solution.py:369
  21.0 0.0 copy-done.1
  21.0 0.0 copy-done
  21.1 275.1 %subspace.1 = (f32[32,1024]{1,0:T(8,128)S(1)}, f32[32,32]{1,0:T(8,128)S(1)}) custom-call(f32[32,1024]{1,0:T(8,128)S(1)} %copy-done, f32[1,1024]{1,0:T(1,128)S(1)} %bitcast.1, bf16[9216,1024]{1,0:T(8,128)(2,1)S(1)} %align.1.weights), custom_call_target="tpu_custom_call" | custom-call | tf_op jit(solution)/shard_map/subspace/pallas_call | solution.py:379
  296.1 0.7 copy.9
  296.8 0.6 copy.10
Async XLA Ops:
  0.6 20.4 %copy-start.1 = (f32[1024]{0:T(1024)S(1)}, f32[1024]{0:T(1024)}, u32[]{:S(2)}) copy-start(f32[1024]{0:T(1024)} %param.6) | copy-start | bytes 12292
  0.6 20.4 %copy-start = (f32[32,1024]{1,0:T(8,128)S(1)}, f32[32,1024]{1,0:T(8,128)}, u32[]{:S(2)}) copy-start(f32[32,1024]{1,0:T(8,128)} %start_ref.1) | copy-start | bytes 393220
  1.4 0.7 copy-start.2

commit v2 on v1

v2 whole, which is shorter than its diff:
```python
import math

import jax
import jax.numpy as jnp
from jax import lax
from jax.experimental import pallas as pl
from jax.experimental.pallas import tpu as pltpu
from jax.sharding import PartitionSpec as P

ITERS = 12
MESH = pl.DeviceIdType.MESH
F32 = jnp.float32
BF16 = jnp.bfloat16
LANE = 128
SIZES = {"yh": 2, "core": 2, "z": 4, "yl": 2, "x": 4}
PHASES = (("yh", "yl", "x"), ("core", "z"))


def split3(value):
    high = value.astype(BF16)
    rest = value - high.astype(F32)
    mid = rest.astype(BF16)
    low = (rest - mid.astype(F32)).astype(BF16)
    return high, mid, low


def coordinates():
    grp, st = lax.axis_index("grp"), lax.axis_index("st")
    return {"yh": grp // 2, "core": grp % 2, "z": st // 8, "yl": (st // 4) % 2, "x": st % 4}


def device_of(at):
    return (at["yh"] * 2 + at["core"], at["z"] * 8 + at["yl"] * 4 + at["x"])


def group(at, names):
    place = 0
    for name in names:
        place = place * SIZES[name] + at[name]
    count = 1
    for name in names:
        count *= SIZES[name]
    others = []
    for code in range(1, count):
        peer, rest = dict(at), code
        for name in reversed(names):
            step = rest % SIZES[name]
            rest //= SIZES[name]
            if step:
                peer[name] = (at[name] + step) % SIZES[name]
        others.append(device_of(peer))
    return place, count, others


def tree_sum(items):
    items = list(items)
    while len(items) > 1:
        items = [a + b for a, b in zip(items[::2], items[1::2])] + ([items[-1]] if len(items) % 2 else [])
    return items[0]


def inverse_factor(gram_rows):
    shape = (8, LANE)
    row8 = lax.broadcasted_iota(jnp.int32, shape, 0)
    lane = lax.broadcasted_iota(jnp.int32, shape, 1)
    g = list(gram_rows)
    inv = [jnp.where(lane % 32 == row8 + 8 * q, F32(1), F32(0)) for q in range(4)]
    out = []
    for p in range(4):
        cols = [[jnp.broadcast_to(g[q][:, 8 * p + k : 8 * p + k + 1], shape) for q in range(p, 4)] for k in range(8)]
        diag = jnp.ones(shape, F32)
        for j in range(8):
            pivot = jnp.broadcast_to(cols[j][0][j : j + 1, :], shape)
            diag = jnp.where(row8 == j, pivot, diag)
            scale = 1.0 / pivot
            factors = [col * scale for col in cols[j]]
            factors[0] = jnp.where(row8 > j, factors[0], F32(0))
            for k in range(j + 1, 8):
                head = jnp.broadcast_to(cols[k][0][j : j + 1, :], shape)
                cols[k] = [col - factor * head for col, factor in zip(cols[k], factors)]
            row_g = jnp.broadcast_to(g[p][j : j + 1, :], shape)
            row_i = jnp.broadcast_to(inv[p][j : j + 1, :], shape)
            for q in range(p, 4):
                if q == p and j == 7:
                    continue
                if q > p or p < 3:
                    g[q] = g[q] - factors[q - p] * row_g
                inv[q] = inv[q] - factors[q - p] * row_i
        out.append(inv[p] * (1.0 / jnp.sqrt(diag)))
    return jnp.concatenate(out, axis=0)


def align(first_ref, width_ref, band_ref, weights, raw, sem):
    blocks, block_rows = raw.shape[0], raw.shape[1]
    window = weights.shape[0]
    loads = []
    for b in range(blocks):
        load = pltpu.make_async_copy(band_ref.at[pl.ds(b * block_rows, block_rows), :], raw.at[b], sem.at[b])
        load.start()
        loads.append(load)
    for b in range(blocks):
        here = slice(b * block_rows, (b + 1) * block_rows)
        loads[b].wait()
        first = first_ref[b] // LANE
        used = width_ref[b] // LANE

        def clear(e, carry, here=here):
            weights[pl.ds(pl.multiple_of(e * LANE, LANE), LANE), here] = jnp.zeros((LANE, block_rows), BF16)
            return carry

        def turn(e, carry, b=b, here=here, first=first):
            piece = raw[b, :, pl.ds(pl.multiple_of(e * LANE, LANE), LANE)]
            weights[pl.ds(pl.multiple_of((first + e) * LANE, LANE), LANE), here] = jnp.transpose(piece)
            return carry

        lax.fori_loop(0, raw.shape[2] // LANE, turn, 0, unroll=8)
        lax.fori_loop(0, first, clear, 0)
        lax.fori_loop(first + used, window // LANE, clear, 0)


def row_scale(stay_ref, weights, scale_ref):
    rows = stay_ref.shape[1]
    ones = jnp.ones((16, rows), BF16)
    total = jnp.zeros((8, rows), F32)
    for d in range(weights.shape[0] // rows):
        total += jnp.dot(ones, weights[d * rows : (d + 1) * rows, :], preferred_element_type=F32)[0:8]
    scale_ref[...] = (1.0 - stay_ref[...]) / total[0:1]


def kernel(
    start_ref, stay_ref, scale_ref, weights,
    out_ref, ritz_ref,
    images, xbuf, left_ref, current, acc,
    sums,
    bulk_send, bulk_recv, row_send, row_recv, sum_send, sum_recv,
):
    count, rows = start_ref.shape
    reach = weights.shape[0] // (2 * rows)
    devices = lax.axis_size("grp") * lax.axis_size("st")
    members = lax.axis_size("st")
    chain = lax.axis_index("grp") * members + lax.axis_index("st")
    at = coordinates()
    groups = [group(at, names) for names in PHASES]

    x = at["x"]

    def chained(by):
        there = lax.rem(chain + by + devices, devices)
        return (there // members, there % members)

    right = device_of({**at, "x": (x + 1) % 4})
    left = device_of({**at, "x": (x + 3) % 4})
    following, preceding = chained(4), chained(-4)
    across = device_of({**at, "x": (x + 2) % 4})
    neighbours = (right, left, across, following, preceding)

    barrier = pltpu.get_barrier_semaphore()
    for device in neighbours:
        pl.semaphore_signal(barrier, inc=1, device_id=device, device_id_type=MESH)
    for device in [device for _, _, others in groups for device in others]:
        pl.semaphore_signal(barrier, inc=1, device_id=device, device_id_type=MESH)

    def pick(condition, first, second):
        return jnp.where(condition, reach + first, reach + second)

    slots = (
        reach,
        pick(x == 0, 3, -1),
        pick(x < 3, 1, -3),
        pick(x < 2, 2, -2),
        reach - 4,
        reach + 4,
        pick(x == 0, -1, 3),
        pick(x == 3, 1, -3),
        pick(x < 2, -2, 2),
    )
    half = count // 2

    def remote(src, dst, send_sem, recv_sem, device):
        return pltpu.make_async_remote_copy(
            src_ref=src, dst_ref=dst, send_sem=send_sem, recv_sem=recv_sem, device_id=device, device_id_type=MESH
        )

    def spread(parity):
        return [
            remote(images.at[parity, 0], images.at[parity, to], bulk_send.at[k], bulk_recv.at[parity, k], device)
            for k, to, device in ((0, 4, following), (1, 5, preceding), (2, 1, right), (3, 2, left))
        ]

    def onward(parity):
        return [
            remote(
                images.at[parity, src, pl.ds(first, half)],
                images.at[parity, 3, pl.ds(first, half)],
                bulk_send.at[k],
                bulk_recv.at[parity, k],
                device,
            )
            for k, src, first, device in ((4, 1, 0, right), (5, 2, half, left))
        ]

    def arrived(parity, k, block, part=None):
        ref = images.at[parity, block] if part is None else images.at[parity, block, part]
        pltpu.make_async_copy(ref, ref, bulk_recv.at[parity, k]).wait()

    before, after = 4, 5
    along = [
        remote(xbuf.at[jnp.where(x >= 2, before, after)], xbuf.at[8], row_send.at[2], row_recv.at[2], across),
        remote(xbuf.at[jnp.where(x == 3, before, after)], xbuf.at[6], row_send.at[0], row_recv.at[0], right),
        remote(xbuf.at[jnp.where(x >= 1, before, after)], xbuf.at[7], row_send.at[1], row_recv.at[1], left),
    ]

    images[0, 0] = start_ref[...]
    row8 = lax.broadcasted_iota(jnp.int32, (count, 8 * count), 0)
    lane8 = lax.broadcasted_iota(jnp.int32, (count, 8 * count), 1)
    kept = jnp.logical_or(lane8 // 32 < 2, lane8 // 32 == 4)
    left_ref[...] = jnp.where(jnp.logical_and(kept, lane8 % 32 == row8), F32(1), F32(0)).astype(BF16)
    pl.semaphore_wait(barrier, len(neighbours) + sum(len(others) for _, _, others in groups))
    for copy in spread(0):
        copy.start()
    arrived(0, 2, 1)
    arrived(0, 3, 2)
    for copy in onward(0):
        copy.start()

    def stored(slot):
        return weights[pl.ds(pl.multiple_of(slot * rows, rows), rows), :]

    def product(block):
        there = chain + (slots[block] - reach)
        valid = jnp.where(jnp.logical_and(there >= 0, there < devices), F32(1), F32(0)).astype(BF16)
        return jnp.dot(xbuf[block] * valid, stored(slots[block]), preferred_element_type=F32)

    def orthonormal(image):
        ih, im, il = split3(image)
        right = jnp.concatenate([ih, im, ih, im, il, ih, il, im], axis=0)
        return jnp.dot(left_ref[...], right, preferred_element_type=F32)

    lane8 = lax.broadcasted_iota(jnp.int32, (8, LANE), 1) // 32
    lane32 = lax.broadcasted_iota(jnp.int32, (count, LANE), 1) // 32

    def packed_product(left3, right3):
        left = jnp.concatenate(left3, axis=0)
        right = jnp.concatenate([piece for piece in right3 for _ in range(4)], axis=0)
        terms = lax.dot_general(left, right, (((1,), (1,)), ((), ())), preferred_element_type=F32)
        full = tree_sum(terms[32 * a : 32 * a + 32, LANE * b : LANE * b + LANE] for a in (2, 1, 0) for b in (2, 1, 0))
        tile = full[0:8]
        for q in range(1, 4):
            tile = jnp.where(lane8 == q, full[8 * q : 8 * q + 8], tile)
        return tile * (1.0 / (rows * devices))

    def unpacked(tile):
        return [tile] + [pltpu.roll(tile, LANE - 32 * q, 1) for q in range(1, 4)]

    stages = len(groups)
    cross = 2 * stages

    def send_all(stage, base, tile):
        place, _, others = groups[stage]
        own_slot = sums.at[base + stage, place]
        own_slot[...] = tile
        for device in others:
            pltpu.make_async_remote_copy(
                src_ref=own_slot,
                dst_ref=own_slot,
                send_sem=sum_send.at[base + stage],
                recv_sem=sum_recv.at[base + stage],
                device_id=device,
                device_id_type=MESH,
            ).start()

    def wait_all(stage, base, sem):
        part = sums.at[base + stage, pl.ds(0, len(groups[stage][2]))]
        pltpu.make_async_copy(part, part, sem.at[base + stage]).wait()

    def received(stage, base):
        wait_all(stage, base, sum_recv)
        return tree_sum(sums[base + stage, i] for i in range(groups[stage][1]))

    def one_step(t, carry):
        parity = t % 2
        final = t == ITERS - 1
        arrived(parity, 0, 4)
        xbuf[4] = orthonormal(images[parity, 4]).astype(BF16)
        arrived(parity, 1, 5)
        xbuf[5] = orthonormal(images[parity, 5]).astype(BF16)
        for copy in along:
            copy.start()
        updated = orthonormal(images[parity, 0])
        current[...] = updated
        xbuf[0] = updated.astype(BF16)
        acc[...] = product(0) + product(4) + product(5)
        xbuf[1] = orthonormal(images[parity, 1]).astype(BF16)
        xbuf[2] = orthonormal(images[parity, 2]).astype(BF16)
        acc[...] += product(1) + product(2)
        arrived(parity, 4, 3, pl.ds(0, half))
        arrived(parity, 5, 3, pl.ds(half, half))
        xbuf[3] = orthonormal(images[parity, 3]).astype(BF16)
        acc[...] += product(3)
        for k, block in ((0, 6), (1, 7), (2, 8)):
            pltpu.make_async_copy(xbuf.at[block], xbuf.at[block], row_recv.at[k]).wait()
        acc[...] += product(6) + product(7) + product(8)
        for copy in spread(parity) + onward(parity) + along:
            copy.wait_send()

        image = stay_ref[...] * current[...] + scale_ref[...] * acc[...]
        images[1 - parity, 0] = image
        pieces = split3(image)
        base = parity * stages
        send_all(0, base, packed_product(pieces, pieces))

        @pl.when(jnp.logical_not(final))
        def _():
            for copy in spread(1 - parity):
                copy.start()

        @pl.when(final)
        def _():
            send_all(0, cross, packed_product(split3(current[...]), pieces))

        for stage in range(1, stages):
            send_all(stage, base, received(stage - 1, base))

            @pl.when(final)
            def _(stage=stage):
                send_all(stage, cross, received(stage - 1, cross))

        gram = unpacked(received(stages - 1, base))

        @pl.when(jnp.logical_not(final))
        def _():
            arrived(1 - parity, 2, 1)
            arrived(1 - parity, 3, 2)
            for copy in onward(1 - parity):
                copy.start()

        for stage in range(stages):
            wait_all(stage, base, sum_send)

        high, mid, low = (piece.astype(F32) for piece in split3(inverse_factor(gram)))
        left_a = jnp.where(lane32 < 2, high, mid)
        left_b = jnp.where(lane32 == 0, high, jnp.where(lane32 == 2, mid, low))
        left_ref[...] = jnp.concatenate([left_a, left_b], axis=1).astype(BF16)
        return carry

    lax.fori_loop(0, ITERS, one_step, 0)

    out_ref[...] = orthonormal(images[ITERS % 2, 0])
    ritz = unpacked(received(stages - 1, cross))
    for q in range(4):
        ritz_ref[8 * q : 8 * q + 8, :] = ritz[q][:, 0:32]
    for stage in range(stages):
        wait_all(stage, cross, sum_send)


def shards(start_vectors, stay, band_blocks, band_start, band_width):
    count, rows = start_vectors.shape
    span = band_blocks.shape[1]
    blocks = band_start.shape[0]
    reach = span // (2 * rows)
    window = 2 * reach + 1
    vmem = pl.BlockSpec(memory_space=pltpu.VMEM)
    smem = pl.BlockSpec(memory_space=pltpu.SMEM)
    most = max(math.prod(SIZES[name] for name in names) for names in PHASES)
    stay = stay.reshape(1, rows)
    chain = lax.axis_index("grp") * lax.axis_size("st") + lax.axis_index("st")
    first = band_start - (chain - reach) * rows
    weights = pl.pallas_call(
        align,
        out_shape=pltpu.VMEM((window * rows, rows), BF16),
        in_specs=[smem, smem, pl.BlockSpec(memory_space=pl.ANY)],
        out_specs=vmem,
        scratch_shapes=[pltpu.VMEM((blocks, rows // blocks, span), BF16), pltpu.SemaphoreType.DMA((blocks,))],
        compiler_params=pltpu.CompilerParams(vmem_limit_bytes=24 * 1024 * 1024),
        name="align",
    )(first, band_width, pltpu.with_memory_space_constraint(band_blocks, pltpu.HBM))
    weights = pltpu.with_memory_space_constraint(weights, pltpu.VMEM)
    scale = pl.pallas_call(
        row_scale,
        out_shape=jax.ShapeDtypeStruct((1, rows), F32),
        in_specs=[vmem, vmem],
        out_specs=vmem,
        compiler_params=pltpu.CompilerParams(vmem_limit_bytes=8 * 1024 * 1024),
        name="row_scale",
    )(stay, weights)
    return pl.pallas_call(
        kernel,
        out_shape=(jax.ShapeDtypeStruct((count, rows), F32), jax.ShapeDtypeStruct((count, count), F32)),
        in_specs=[vmem, vmem, vmem, vmem],
        out_specs=(vmem, vmem),
        scratch_shapes=[
            pltpu.VMEM((2, 6, count, rows), F32),
            pltpu.VMEM((window, count, rows), BF16),
            pltpu.VMEM((count, 8 * count), BF16),
            pltpu.VMEM((count, rows), F32),
            pltpu.VMEM((count, rows), F32),
            pltpu.VMEM((3 * len(PHASES), most, 8, LANE), F32),
            pltpu.SemaphoreType.DMA((6,)),
            pltpu.SemaphoreType.DMA((2, 6)),
            pltpu.SemaphoreType.DMA((3,)),
            pltpu.SemaphoreType.DMA((3,)),
            pltpu.SemaphoreType.DMA((3 * len(PHASES),)),
            pltpu.SemaphoreType.DMA((3 * len(PHASES),)),
        ],
        compiler_params=pltpu.CompilerParams(
            collective_id=0, has_side_effects=True, vmem_limit_bytes=12 * 1024 * 1024
        ),
        name="subspace",
    )(start_vectors, stay, scale, weights)


def solution(mesh):
    placed = (
        P(None, ("grp", "st")),
        P(("grp", "st")),
        P(("grp", "st"), None),
        P(("grp", "st")),
        P(("grp", "st")),
    )
    return jax.shard_map(
        shards, mesh=mesh, in_specs=placed, out_specs=(P(None, ("grp", "st")), P()), check_vma=False
    )
```

time: 298 us -> 234 us (0.79)
  Pallas kernels: 294 us -> 231 us
    pallas_call x1, Pallas kernels: 275 us -> 218 us  [shards(): pl.pallas_call(kernel, out_shape=(jax.ShapeDtypeStruct((count, rows), F32...]
    pallas_call x1, Pallas kernels: 19 us -> 9.72 us  [shards(): pl.pallas_call(align, out_shape=pltpu.VMEM((window * rows, rows), BF16),...]
where the time goes in v2:
time: 234 us
  Pallas kernels  231 us (99%)
    pallas_call x1, Pallas kernels, shards(): pl.pallas_call(kernel, out_shape=(jax.ShapeDtypeStruct((count, rows), F32...  218 us
    pallas_call x1, Pallas kernels, shards(): pl.pallas_call(align, out_shape=pltpu.VMEM((window * rows, rows), BF16),...  9.72 us

profile of v2, /device:TPU:1, one launch (start us, length us, event | category | flops | bytes accessed | tf_op | source)
XLA Modules:
  0.0 234.0 jit_solution(15156339803661820407)
XLA Ops:
  0.6 0.0 copy-start.1
  0.6 0.7 broadcast_subtract_fusion.first_ref
  1.3 0.0 copy-start.2
  1.3 0.7 copy-done.2
  2.0 0.0 copy-start
  2.0 9.7 %align.1.weights = bf16[9216,1024]{1,0:T(8,128)(2,1)S(1)} custom-call(s32[4]{0:T(128)S(1)} %broadcast_subtract_fusion.first_ref, s32[4]{0:T(128)S(1)} %copy-done.2, bf16[1024,8192]{1,0:T(8,128)(2,1)} %band_ref.1), custom_call_target="tpu_custom_call" | custom-call | tf_op jit(solution)/shard_map/align/pallas_call | solution.py:368
  11.7 0.0 copy-done.1
  11.7 2.5 %row_scale.1.scale_ref = f32[1,1024]{1,0:T(1,128)S(1)} custom-call(f32[1,1024]{1,0:T(1,128)S(1)} %bitcast.1, bf16[9216,1024]{1,0:T(8,128)(2,1)S(1)} %align.1.weights), custom_call_target="tpu_custom_call" | custom-call | tf_op jit(solution)/shard_map/row_scale/pallas_call | solution.py:378
  14.2 0.0 copy-done
  14.2 218.5 %subspace.1 = (f32[32,1024]{1,0:T(8,128)S(1)}, f32[32,32]{1,0:T(8,128)S(1)}) custom-call(f32[32,1024]{1,0:T(8,128)S(1)} %copy-done, f32[1,1024]{1,0:T(1,128)S(1)} %bitcast.2, f32[1,1024]{1,0:T(1,128)S(1)} %row_scale.1.scale_ref, bf16[9216,1024]{1,0:T(8,128)(2,1)S(1)} %align.1.weights), custom_call_target="tpu_custom_call" | custom-call | tf_op jit(solution)/shard_map/subspace/pallas_call | solution.py:386
  232.7 0.7 copy.9
  233.4 0.6 copy.10
Async XLA Ops:
  0.6 11.1 %copy-start.1 = (f32[1024]{0:T(1024)S(1)}, f32[1024]{0:T(1024)}, u32[]{:S(2)}) copy-start(f32[1024]{0:T(1024)} %param.6) | copy-start | bytes 12292
  1.3 0.7 copy-start.2
  2.0 12.3 %copy-start = (f32[32,1024]{1,0:T(8,128)S(1)}, f32[32,1024]{1,0:T(8,128)}, u32[]{:S(2)}) copy-start(f32[32,1024]{1,0:T(8,128)} %start_ref.1) | copy-start | bytes 393220

commit v3 on v2

--- a/solution.py
+++ b/solution.py
@@ -90,41 +90,39 @@
     return jnp.concatenate(out, axis=0)
 
 
-def align(first_ref, width_ref, band_ref, weights, raw, sem):
-    blocks, block_rows = raw.shape[0], raw.shape[1]
+def align(stay_ref, first_ref, width_ref, band_ref, weights, scale_ref, raw, sem):
+    chunks, chunk_rows = raw.shape[0], raw.shape[1]
     window = weights.shape[0]
-    loads = []
-    for b in range(blocks):
-        load = pltpu.make_async_copy(band_ref.at[pl.ds(b * block_rows, block_rows), :], raw.at[b], sem.at[b])
-        load.start()
-        loads.append(load)
-    for b in range(blocks):
-        here = slice(b * block_rows, (b + 1) * block_rows)
-        loads[b].wait()
-        first = first_ref[b] // LANE
-        used = width_ref[b] // LANE
+    ahead = 3
+    loads = [
+        pltpu.make_async_copy(band_ref.at[pl.ds(c * chunk_rows, chunk_rows), :], raw.at[c], sem.at[c])
+        for c in range(chunks)
+    ]
+    for c in range(ahead):
+        loads[c].start()
+    for c in range(chunks):
+        here = slice(c * chunk_rows, (c + 1) * chunk_rows)
+        loads[c].wait()
+        if c + ahead < chunks:
+            loads[c + ahead].start()
+        block = c * first_ref.shape[0] // chunks
+        first = first_ref[block] // LANE
+        used = width_ref[block] // LANE
 
         def clear(e, carry, here=here):
-            weights[pl.ds(pl.multiple_of(e * LANE, LANE), LANE), here] = jnp.zeros((LANE, block_rows), BF16)
+            weights[pl.ds(pl.multiple_of(e * LANE, LANE), LANE), here] = jnp.zeros((LANE, chunk_rows), BF16)
             return carry
 
-        def turn(e, carry, b=b, here=here, first=first):
-            piece = raw[b, :, pl.ds(pl.multiple_of(e * LANE, LANE), LANE)]
-            weights[pl.ds(pl.multiple_of((first + e) * LANE, LANE), LANE), here] = jnp.transpose(piece)
-            return carry
-
-        lax.fori_loop(0, raw.shape[2] // LANE, turn, 0, unroll=8)
+        def turn(e, total, c=c, here=here, first=first, used=used):
+            piece = jnp.transpose(raw[c, :, pl.ds(pl.multiple_of(e * LANE, LANE), LANE)])
+            weights[pl.ds(pl.multiple_of((first + e) * LANE, LANE), LANE), here] = piece
+            part = tree_sum(piece[r : r + 16].astype(F32) for r in range(0, LANE, 16))
+            return total + jnp.where(e < used, part, F32(0))
+
+        total = lax.fori_loop(0, raw.shape[2] // LANE, turn, jnp.zeros((16, chunk_rows), F32), unroll=8)
         lax.fori_loop(0, first, clear, 0)
         lax.fori_loop(first + used, window // LANE, clear, 0)
-
-
-def row_scale(stay_ref, weights, scale_ref):
-    rows = stay_ref.shape[1]
-    ones = jnp.ones((16, rows), BF16)
-    total = jnp.zeros((8, rows), F32)
-    for d in range(weights.shape[0] // rows):
-        total += jnp.dot(ones, weights[d * rows : (d + 1) * rows, :], preferred_element_type=F32)[0:8]
-    scale_ref[...] = (1.0 - stay_ref[...]) / total[0:1]
+        scale_ref[:, here] = (1.0 - stay_ref[:, here]) / jnp.sum(total, axis=0, keepdims=True)
 
 
 def kernel(
@@ -151,8 +149,7 @@
     right = device_of({**at, "x": (x + 1) % 4})
     left = device_of({**at, "x": (x + 3) % 4})
     following, preceding = chained(4), chained(-4)
-    across = device_of({**at, "x": (x + 2) % 4})
-    neighbours = (right, left, across, following, preceding)
+    neighbours = (right, left, following, preceding)
 
     barrier = pltpu.get_barrier_semaphore()
     for device in neighbours:
@@ -184,7 +181,7 @@
     def spread(parity):
         return [
             remote(images.at[parity, 0], images.at[parity, to], bulk_send.at[k], bulk_recv.at[parity, k], device)
-            for k, to, device in ((0, 4, following), (1, 5, preceding), (2, 1, right), (3, 2, left))
+            for k, to, device in ((2, 1, right), (3, 2, left), (0, 4, following), (1, 5, preceding))
         ]
 
     def onward(parity):
@@ -205,10 +202,11 @@
 
     before, after = 4, 5
     along = [
-        remote(xbuf.at[jnp.where(x >= 2, before, after)], xbuf.at[8], row_send.at[2], row_recv.at[2], across),
         remote(xbuf.at[jnp.where(x == 3, before, after)], xbuf.at[6], row_send.at[0], row_recv.at[0], right),
         remote(xbuf.at[jnp.where(x >= 1, before, after)], xbuf.at[7], row_send.at[1], row_recv.at[1], left),
     ]
+    same_x = tuple(jnp.where(x < 2, a, b) for a, b in zip(following, preceding))
+    over = remote(xbuf.at[3], xbuf.at[8], row_send.at[2], row_recv.at[2], same_x)
 
     images[0, 0] = start_ref[...]
     row8 = lax.broadcasted_iota(jnp.int32, (count, 8 * count), 0)
@@ -281,26 +279,27 @@
         parity = t % 2
         final = t == ITERS - 1
         arrived(parity, 0, 4)
+        arrived(parity, 1, 5)
         xbuf[4] = orthonormal(images[parity, 4]).astype(BF16)
-        arrived(parity, 1, 5)
         xbuf[5] = orthonormal(images[parity, 5]).astype(BF16)
         for copy in along:
             copy.start()
         updated = orthonormal(images[parity, 0])
         current[...] = updated
         xbuf[0] = updated.astype(BF16)
-        acc[...] = product(0) + product(4) + product(5)
-        xbuf[1] = orthonormal(images[parity, 1]).astype(BF16)
-        xbuf[2] = orthonormal(images[parity, 2]).astype(BF16)
-        acc[...] += product(1) + product(2)
         arrived(parity, 4, 3, pl.ds(0, half))
         arrived(parity, 5, 3, pl.ds(half, half))
         xbuf[3] = orthonormal(images[parity, 3]).astype(BF16)
-        acc[...] += product(3)
-        for k, block in ((0, 6), (1, 7), (2, 8)):
+        over.start()
+        xbuf[1] = orthonormal(images[parity, 1]).astype(BF16)
+        xbuf[2] = orthonormal(images[parity, 2]).astype(BF16)
+        acc[...] = tree_sum(product(block) for block in range(6))
+        for k, block in ((0, 6), (1, 7)):
             pltpu.make_async_copy(xbuf.at[block], xbuf.at[block], row_recv.at[k]).wait()
-        acc[...] += product(6) + product(7) + product(8)
-        for copy in spread(parity) + onward(parity) + along:
+        acc[...] += product(6) + product(7)
+        pltpu.make_async_copy(xbuf.at[8], xbuf.at[8], row_recv.at[2]).wait()
+        acc[...] += product(8)
+        for copy in spread(parity) + onward(parity) + along + [over]:
             copy.wait_send()
 
         image = stay_ref[...] * current[...] + scale_ref[...] * acc[...]
@@ -365,24 +364,16 @@
     stay = stay.reshape(1, rows)
     chain = lax.axis_index("grp") * lax.axis_size("st") + lax.axis_index("st")
     first = band_start - (chain - reach) * rows
-    weights = pl.pallas_call(
+    weights, scale = pl.pallas_call(
         align,
-        out_shape=pltpu.VMEM((window * rows, rows), BF16),
-        in_specs=[smem, smem, pl.BlockSpec(memory_space=pl.ANY)],
-        out_specs=vmem,
-        scratch_shapes=[pltpu.VMEM((blocks, rows // blocks, span), BF16), pltpu.SemaphoreType.DMA((blocks,))],
+        out_shape=(pltpu.VMEM((window * rows, rows), BF16), jax.ShapeDtypeStruct((1, rows), F32)),
+        in_specs=[vmem, smem, smem, pl.BlockSpec(memory_space=pl.ANY)],
+        out_specs=(vmem, vmem),
+        scratch_shapes=[pltpu.VMEM((8, rows // 8, span), BF16), pltpu.SemaphoreType.DMA((8,))],
         compiler_params=pltpu.CompilerParams(vmem_limit_bytes=24 * 1024 * 1024),
         name="align",
-    )(first, band_width, pltpu.with_memory_space_constraint(band_blocks, pltpu.HBM))
+    )(stay, first, band_width, pltpu.with_memory_space_constraint(band_blocks, pltpu.HBM))
     weights = pltpu.with_memory_space_constraint(weights, pltpu.VMEM)
-    scale = pl.pallas_call(
-        row_scale,
-        out_shape=jax.ShapeDtypeStruct((1, rows), F32),
-        in_specs=[vmem, vmem],
-        out_specs=vmem,
-        compiler_params=pltpu.CompilerParams(vmem_limit_bytes=8 * 1024 * 1024),
-        name="row_scale",
-    )(stay, weights)
     return pl.pallas_call(
         kernel,
         out_shape=(jax.ShapeDtypeStruct((count, rows), F32), jax.ShapeDtypeStruct((count, count), F32)),

time: 234 us -> 245 us (1.047)
  Pallas kernels: 231 us -> 240 us
    pallas_call x1, Pallas kernels: 218 us -> 227 us  [shards(): pl.pallas_call(kernel, out_shape=(jax.ShapeDtypeStruct((count, rows), F32...]
    pallas_call x2 -> x1, Pallas kernels: 12.3 us -> 13.2 us  [shards(): pl.pallas_call(align, out_shape=(pltpu.VMEM((window * rows, rows), BF16),...]
where the time goes in v3:
time: 245 us
  Pallas kernels  240 us (98%)
  local copies, waits for them, and re-layouts  3.5 us (1%)
    pallas_call x1, Pallas kernels, shards(): pl.pallas_call(kernel, out_shape=(jax.ShapeDtypeStruct((count, rows), F32...  227 us
    pallas_call x1, Pallas kernels, shards(): pl.pallas_call(align, out_shape=(pltpu.VMEM((window * rows, rows), BF16),...  13.2 us

profile of v3, /device:TPU:1, one launch (start us, length us, event | category | flops | bytes accessed | tf_op | source)
XLA Modules:
  0.0 244.6 jit_solution(13792258518938867083)
XLA Ops:
  0.6 0.7 broadcast_subtract_fusion.first_ref
  1.3 0.0 copy-start.1
  1.3 0.7 copy-done.1
  2.0 0.0 copy-start.2
  2.0 0.7 copy-done.2
  2.6 13.2 %align.1 = (bf16[9216,1024]{1,0:T(8,128)(2,1)S(1)}, f32[1,1024]{1,0:T(1,128)S(1)}) custom-call(f32[1,1024]{1,0:T(1,128)S(1)} %bitcast.1, s32[4]{0:T(128)S(1)} %broadcast_subtract_fusion.first_ref, s32[4]{0:T(128)S(1)} %copy-done.2, bf16[1024,8192]{1,0:T(8,128)(2,1)} %band_ref.1), custom_call_target="tpu_custom_call" | custom-call | tf_op jit(solution)/shard_map/align/pallas_call | solution.py:367
  15.8 0.0 copy-start
  15.8 0.9 copy-done
  16.7 226.6 %subspace.1 = (f32[32,1024]{1,0:T(8,128)S(1)}, f32[32,32]{1,0:T(8,128)S(1)}) custom-call(f32[32,1024]{1,0:T(8,128)S(1)} %copy-done, f32[1,1024]{1,0:T(1,128)S(1)} %bitcast.2, f32[1,1024]{1,0:T(1,128)S(1)} %get-tuple-element.4.scale_ref, bf16[9216,1024]{1,0:T(8,128)(2,1)S(1)} %get-tuple-element.5.weights), custom_call_target="tpu_custom_call" | custom-call | tf_op jit(solution)/shard_map/subspace/pallas_call | solution.py:377
  243.3 0.7 copy.9
  244.0 0.6 copy.10
Async XLA Ops:
  1.3 0.7 copy-start.1
  2.0 0.7 copy-start.2
  15.8 0.9 copy-start

commit v4 on v2

--- a/solution.py
+++ b/solution.py
@@ -59,7 +59,7 @@
     return items[0]
 
 
-def inverse_factor(gram_rows):
+def inverse_factor(gram_rows, midway):
     shape = (8, LANE)
     row8 = lax.broadcasted_iota(jnp.int32, shape, 0)
     lane = lax.broadcasted_iota(jnp.int32, shape, 1)
@@ -67,6 +67,8 @@
     inv = [jnp.where(lane % 32 == row8 + 8 * q, F32(1), F32(0)) for q in range(4)]
     out = []
     for p in range(4):
+        if p == 2:
+            midway()
         cols = [[jnp.broadcast_to(g[q][:, 8 * p + k : 8 * p + k + 1], shape) for q in range(p, 4)] for k in range(8)]
         diag = jnp.ones(shape, F32)
         for j in range(8):
@@ -90,19 +92,36 @@
     return jnp.concatenate(out, axis=0)
 
 
-def align(first_ref, width_ref, band_ref, weights, raw, sem):
+def align(start_ref, width_ref, band_ref, weights, raw, starts, widths, sem, small_sem):
     blocks, block_rows = raw.shape[0], raw.shape[1]
-    window = weights.shape[0]
-    loads = []
-    for b in range(blocks):
-        load = pltpu.make_async_copy(band_ref.at[pl.ds(b * block_rows, block_rows), :], raw.at[b], sem.at[b])
+    window, rows = weights.shape
+    chain = lax.axis_index("grp") * lax.axis_size("st") + lax.axis_index("st")
+    ahead, pieces = 2, 2
+    part = block_rows // pieces
+    loads = [
+        pltpu.make_async_copy(
+            band_ref.at[pl.ds(k * part, part), :], raw.at[k // pieces, pl.ds((k % pieces) * part, part)], sem.at[k]
+        )
+        for k in range(blocks * pieces)
+    ]
+    for load in loads[:ahead]:
         load.start()
-        loads.append(load)
+    small = [
+        pltpu.make_async_copy(start_ref, starts, small_sem.at[0]),
+        pltpu.make_async_copy(width_ref, widths, small_sem.at[1]),
+    ]
+    for copy in small:
+        copy.start()
+    for copy in small:
+        copy.wait()
     for b in range(blocks):
         here = slice(b * block_rows, (b + 1) * block_rows)
-        loads[b].wait()
-        first = first_ref[b] // LANE
-        used = width_ref[b] // LANE
+        for k in range(b * pieces, (b + 1) * pieces):
+            loads[k].wait()
+            if k + ahead < len(loads):
+                loads[k + ahead].start()
+        first = (starts[b] - chain * rows) // LANE + (window - rows) // (2 * LANE)
+        used = widths[b] // LANE
 
         def clear(e, carry, here=here):
             weights[pl.ds(pl.multiple_of(e * LANE, LANE), LANE), here] = jnp.zeros((LANE, block_rows), BF16)
@@ -118,21 +137,21 @@
         lax.fori_loop(first + used, window // LANE, clear, 0)
 
 
-def row_scale(stay_ref, weights, scale_ref):
-    rows = stay_ref.shape[1]
+def row_sums(weights, sums_ref):
+    rows = sums_ref.shape[1]
     ones = jnp.ones((16, rows), BF16)
     total = jnp.zeros((8, rows), F32)
     for d in range(weights.shape[0] // rows):
         total += jnp.dot(ones, weights[d * rows : (d + 1) * rows, :], preferred_element_type=F32)[0:8]
-    scale_ref[...] = (1.0 - stay_ref[...]) / total[0:1]
+    sums_ref[...] = total[0:1]
 
 
 def kernel(
-    start_ref, stay_ref, scale_ref, weights,
+    start_ref, stay_in, rowsum_ref, weights,
     out_ref, ritz_ref,
-    images, xbuf, left_ref, current, acc,
+    stay_ref, scale_ref, images, xbuf, left_ref, current, acc,
     sums,
-    bulk_send, bulk_recv, row_send, row_recv, sum_send, sum_recv,
+    bulk_send, bulk_recv, row_send, row_recv, sum_send, sum_recv, input_sem,
 ):
     count, rows = start_ref.shape
     reach = weights.shape[0] // (2 * rows)
@@ -141,6 +160,13 @@
     chain = lax.axis_index("grp") * members + lax.axis_index("st")
     at = coordinates()
     groups = [group(at, names) for names in PHASES]
+
+    inputs = [
+        pltpu.make_async_copy(start_ref, images.at[0, 0], input_sem.at[0]),
+        pltpu.make_async_copy(stay_in, stay_ref, input_sem.at[1]),
+    ]
+    for copy in inputs:
+        copy.start()
 
     x = at["x"]
 
@@ -210,14 +236,16 @@
         remote(xbuf.at[jnp.where(x >= 1, before, after)], xbuf.at[7], row_send.at[1], row_recv.at[1], left),
     ]
 
-    images[0, 0] = start_ref[...]
     row8 = lax.broadcasted_iota(jnp.int32, (count, 8 * count), 0)
     lane8 = lax.broadcasted_iota(jnp.int32, (count, 8 * count), 1)
     kept = jnp.logical_or(lane8 // 32 < 2, lane8 // 32 == 4)
     left_ref[...] = jnp.where(jnp.logical_and(kept, lane8 % 32 == row8), F32(1), F32(0)).astype(BF16)
     pl.semaphore_wait(barrier, len(neighbours) + sum(len(others) for _, _, others in groups))
+    for copy in inputs:
+        copy.wait()
     for copy in spread(0):
         copy.start()
+    scale_ref[...] = (1.0 - stay_ref[...]) / rowsum_ref[...]
     arrived(0, 2, 1)
     arrived(0, 3, 2)
     for copy in onward(0):
@@ -307,11 +335,18 @@
         images[1 - parity, 0] = image
         pieces = split3(image)
         base = parity * stages
-        send_all(0, base, packed_product(pieces, pieces))
+        early = spread(1 - parity)
 
         @pl.when(jnp.logical_not(final))
         def _():
-            for copy in spread(1 - parity):
+            for copy in early[:2]:
+                copy.start()
+
+        send_all(0, base, packed_product(pieces, pieces))
+
+        @pl.when(jnp.logical_not(final))
+        def _():
+            for copy in early[2:]:
                 copy.start()
 
         @pl.when(final)
@@ -327,17 +362,18 @@
 
         gram = unpacked(received(stages - 1, base))
 
-        @pl.when(jnp.logical_not(final))
-        def _():
-            arrived(1 - parity, 2, 1)
-            arrived(1 - parity, 3, 2)
-            for copy in onward(1 - parity):
-                copy.start()
+        def pass_on():
+            @pl.when(jnp.logical_not(final))
+            def _():
+                arrived(1 - parity, 2, 1)
+                arrived(1 - parity, 3, 2)
+                for copy in onward(1 - parity):
+                    copy.start()
 
         for stage in range(stages):
             wait_all(stage, base, sum_send)
 
-        high, mid, low = (piece.astype(F32) for piece in split3(inverse_factor(gram)))
+        high, mid, low = (piece.astype(F32) for piece in split3(inverse_factor(gram, pass_on)))
         left_a = jnp.where(lane32 < 2, high, mid)
         left_b = jnp.where(lane32 == 0, high, jnp.where(lane32 == 2, mid, low))
         left_ref[...] = jnp.concatenate([left_a, left_b], axis=1).astype(BF16)
@@ -360,35 +396,45 @@
     reach = span // (2 * rows)
     window = 2 * reach + 1
     vmem = pl.BlockSpec(memory_space=pltpu.VMEM)
-    smem = pl.BlockSpec(memory_space=pltpu.SMEM)
     most = max(math.prod(SIZES[name] for name in names) for names in PHASES)
     stay = stay.reshape(1, rows)
-    chain = lax.axis_index("grp") * lax.axis_size("st") + lax.axis_index("st")
-    first = band_start - (chain - reach) * rows
+    hbm = pl.BlockSpec(memory_space=pl.ANY)
+
+    def held(array):
+        return pltpu.with_memory_space_constraint(array, pltpu.HBM)
+
     weights = pl.pallas_call(
         align,
         out_shape=pltpu.VMEM((window * rows, rows), BF16),
-        in_specs=[smem, smem, pl.BlockSpec(memory_space=pl.ANY)],
+        in_specs=[hbm, hbm, hbm],
         out_specs=vmem,
-        scratch_shapes=[pltpu.VMEM((blocks, rows // blocks, span), BF16), pltpu.SemaphoreType.DMA((blocks,))],
+        scratch_shapes=[
+            pltpu.VMEM((blocks, rows // blocks, span), BF16),
+            pltpu.SMEM((blocks,), jnp.int32),
+            pltpu.SMEM((blocks,), jnp.int32),
+            pltpu.SemaphoreType.DMA((2 * blocks,)),
+            pltpu.SemaphoreType.DMA((2,)),
+        ],
         compiler_params=pltpu.CompilerParams(vmem_limit_bytes=24 * 1024 * 1024),
         name="align",
-    )(first, band_width, pltpu.with_memory_space_constraint(band_blocks, pltpu.HBM))
+    )(held(band_start), held(band_width), held(band_blocks))
     weights = pltpu.with_memory_space_constraint(weights, pltpu.VMEM)
-    scale = pl.pallas_call(
-        row_scale,
+    rowsum = pl.pallas_call(
+        row_sums,
         out_shape=jax.ShapeDtypeStruct((1, rows), F32),
-        in_specs=[vmem, vmem],
+        in_specs=[vmem],
         out_specs=vmem,
         compiler_params=pltpu.CompilerParams(vmem_limit_bytes=8 * 1024 * 1024),
-        name="row_scale",
-    )(stay, weights)
+        name="row_sums",
+    )(weights)
     return pl.pallas_call(
         kernel,
         out_shape=(jax.ShapeDtypeStruct((count, rows), F32), jax.ShapeDtypeStruct((count, count), F32)),
-        in_specs=[vmem, vmem, vmem, vmem],
+        in_specs=[hbm, hbm, vmem, vmem],
         out_specs=(vmem, vmem),
         scratch_shapes=[
+            pltpu.VMEM((1, rows), F32),
+            pltpu.VMEM((1, rows), F32),
             pltpu.VMEM((2, 6, count, rows), F32),
             pltpu.VMEM((window, count, rows), BF16),
             pltpu.VMEM((count, 8 * count), BF16),
@@ -401,12 +447,13 @@
             pltpu.SemaphoreType.DMA((3,)),
             pltpu.SemaphoreType.DMA((3 * len(PHASES),)),
             pltpu.SemaphoreType.DMA((3 * len(PHASES),)),
+            pltpu.SemaphoreType.DMA((2,)),
         ],
         compiler_params=pltpu.CompilerParams(
             collective_id=0, has_side_effects=True, vmem_limit_bytes=12 * 1024 * 1024
         ),
         name="subspace",
-    )(start_vectors, stay, scale, weights)
+    )(held(start_vectors), held(stay), rowsum, weights)
 
 
 def solution(mesh):

time: 234 us -> 275 us (1.18)
  Pallas kernels: 231 us -> 273 us
    pallas_call x1, Pallas kernels: 218 us -> 260 us  [shards(): pl.pallas_call(kernel, out_shape=(jax.ShapeDtypeStruct((count, rows), F32...]
where the time goes in v4:
time: 275 us
  Pallas kernels  273 us (99%)
    pallas_call x1, Pallas kernels, shards(): pl.pallas_call(kernel, out_shape=(jax.ShapeDtypeStruct((count, rows), F32...  260 us
    pallas_call x1, Pallas kernels, shards(): pl.pallas_call(align, out_shape=pltpu.VMEM((window * rows, rows), BF16),...  10 us

profile of v4, /device:TPU:1, one launch (start us, length us, event | category | flops | bytes accessed | tf_op | source)
XLA Modules:
  0.0 274.5 jit_solution(17673161988143536619)
XLA Ops:
  0.6 10.0 %align.1.weights = bf16[9216,1024]{1,0:T(8,128)(2,1)S(1)} custom-call(s32[4]{0:T(128)} %start_ref.2, s32[4]{0:T(128)} %width_ref.1, bf16[1024,8192]{1,0:T(8,128)(2,1)} %band_ref.1), custom_call_target="tpu_custom_call" | custom-call | tf_op jit(solution)/shard_map/align/pallas_call | solution.py:406
  10.6 2.5 row_sums.1.rowsum_ref
  13.2 260.1 %subspace.1 = (f32[32,1024]{1,0:T(8,128)S(1)}, f32[32,32]{1,0:T(8,128)S(1)}) custom-call(f32[32,1024]{1,0:T(8,128)} %start_ref.3, f32[1,1024]{1,0:T(1,128)} %bitcast.1, f32[1,1024]{1,0:T(1,128)S(1)} %row_sums.1.rowsum_ref, bf16[9216,1024]{1,0:T(8,128)(2,1)S(1)} %align.1.weights), custom_call_target="tpu_custom_call" | custom-call | tf_op jit(solution)/shard_map/subspace/pallas_call | solution.py:430
  273.3 0.7 copy.9
  273.9 0.6 copy.10

commit v5 on v4

--- a/solution.py
+++ b/solution.py
@@ -65,30 +65,60 @@
     lane = lax.broadcasted_iota(jnp.int32, shape, 1)
     g = list(gram_rows)
     inv = [jnp.where(lane % 32 == row8 + 8 * q, F32(1), F32(0)) for q in range(4)]
+
+    def whole(tile, i):
+        return jnp.broadcast_to(tile[i : i + 1, :], shape)
+
     out = []
     for p in range(4):
         if p == 2:
             midway()
         cols = [[jnp.broadcast_to(g[q][:, 8 * p + k : 8 * p + k + 1], shape) for q in range(p, 4)] for k in range(8)]
-        diag = jnp.ones(shape, F32)
+        e = {(i, k): whole(cols[k][0], i) for k in range(8) for i in range(k, 8)}
+        rows_g = [whole(g[p], i) for i in range(8)] if p < 3 else []
+        rows_i = [whole(inv[p], i) for i in range(8)]
+        m, scale = {}, []
         for j in range(8):
-            pivot = jnp.broadcast_to(cols[j][0][j : j + 1, :], shape)
-            diag = jnp.where(row8 == j, pivot, diag)
-            scale = 1.0 / pivot
-            factors = [col * scale for col in cols[j]]
-            factors[0] = jnp.where(row8 > j, factors[0], F32(0))
+            scale.append(1.0 / e[j, j])
+            for i in range(j + 1, 8):
+                m[i, j] = e[i, j] * scale[j]
             for k in range(j + 1, 8):
-                head = jnp.broadcast_to(cols[k][0][j : j + 1, :], shape)
-                cols[k] = [col - factor * head for col, factor in zip(cols[k], factors)]
-            row_g = jnp.broadcast_to(g[p][j : j + 1, :], shape)
-            row_i = jnp.broadcast_to(inv[p][j : j + 1, :], shape)
-            for q in range(p, 4):
-                if q == p and j == 7:
-                    continue
-                if q > p or p < 3:
-                    g[q] = g[q] - factors[q - p] * row_g
-                inv[q] = inv[q] - factors[q - p] * row_i
-        out.append(inv[p] * (1.0 / jnp.sqrt(diag)))
+                for i in range(k, 8):
+                    e[i, k] = e[i, k] - m[i, j] * e[k, j]
+        n = {}
+        for i in range(8):
+            for j in range(i):
+                total = m[i, j]
+                for k in range(j + 1, i):
+                    total = total + m[i, k] * n[k, j]
+                n[i, j] = -total
+
+        def finished(rows):
+            done = []
+            for i in range(8):
+                total = rows[i]
+                for j in range(i):
+                    total = total + n[i, j] * rows[j]
+                done.append(total)
+            return done
+
+        done_g, done_i = finished(rows_g) if p < 3 else [], finished(rows_i)
+        for q in range(p + 1, 4):
+            below = [cols[k][q - p] for k in range(8)]
+            change_g, change_i = [], []
+            for j in range(8):
+                factor = below[j] * scale[j]
+                for k in range(j + 1, 8):
+                    below[k] = below[k] - factor * e[k, j]
+                change_g.append(factor * done_g[j])
+                change_i.append(factor * done_i[j])
+            g[q] = g[q] - tree_sum(change_g)
+            inv[q] = inv[q] - tree_sum(change_i)
+        rows_done, diag = done_i[0], e[0, 0]
+        for j in range(1, 8):
+            rows_done = jnp.where(row8 == j, done_i[j], rows_done)
+            diag = jnp.where(row8 == j, e[j, j], diag)
+        out.append(rows_done * (1.0 / jnp.sqrt(diag)))
     return jnp.concatenate(out, axis=0)
 
 
@@ -337,16 +367,11 @@
         base = parity * stages
         early = spread(1 - parity)
 
+        send_all(0, base, packed_product(pieces, pieces))
+
         @pl.when(jnp.logical_not(final))
         def _():
-            for copy in early[:2]:
-                copy.start()
-
-        send_all(0, base, packed_product(pieces, pieces))
-
-        @pl.when(jnp.logical_not(final))
-        def _():
-            for copy in early[2:]:
+            for copy in early:
                 copy.start()
 
         @pl.when(final)

time: 275 us -> 240 us (0.87)
  Pallas kernels: 273 us -> 238 us
    pallas_call x1, Pallas kernels: 260 us -> 226 us  [shards(): pl.pallas_call(kernel, out_shape=(jax.ShapeDtypeStruct((count, rows), F32...]
where the time goes in v5:
time: 240 us
  Pallas kernels  238 us (99%)
    pallas_call x1, Pallas kernels, shards(): pl.pallas_call(kernel, out_shape=(jax.ShapeDtypeStruct((count, rows), F32...  226 us
    pallas_call x1, Pallas kernels, shards(): pl.pallas_call(align, out_shape=pltpu.VMEM((window * rows, rows), BF16),...  9.93 us

profile of v5, /device:TPU:1, one launch (start us, length us, event | category | flops | bytes accessed | tf_op | source)
XLA Modules:
  0.0 240.1 jit_solution(11120071861927931588)
XLA Ops:
  0.6 9.9 %align.1.weights = bf16[9216,1024]{1,0:T(8,128)(2,1)S(1)} custom-call(s32[4]{0:T(128)} %start_ref.2, s32[4]{0:T(128)} %width_ref.1, bf16[1024,8192]{1,0:T(8,128)(2,1)} %band_ref.1), custom_call_target="tpu_custom_call" | custom-call | tf_op jit(solution)/shard_map/align/pallas_call | solution.py:431
  10.6 2.5 %row_sums.1.rowsum_ref = f32[1,1024]{1,0:T(1,128)S(1)} custom-call(bf16[9216,1024]{1,0:T(8,128)(2,1)S(1)} %align.1.weights), custom_call_target="tpu_custom_call" | custom-call | tf_op jit(solution)/shard_map/row_sums/pallas_call | solution.py:447
  13.1 225.8 %subspace.1 = (f32[32,1024]{1,0:T(8,128)S(1)}, f32[32,32]{1,0:T(8,128)S(1)}) custom-call(f32[32,1024]{1,0:T(8,128)} %start_ref.3, f32[1,1024]{1,0:T(1,128)} %bitcast.1, f32[1,1024]{1,0:T(1,128)S(1)} %row_sums.1.rowsum_ref, bf16[9216,1024]{1,0:T(8,128)(2,1)S(1)} %align.1.weights), custom_call_target="tpu_custom_call" | custom-call | tf_op jit(solution)/shard_map/subspace/pallas_call | solution.py:455
  238.9 0.7 copy.9
  239.5 0.6 copy.10

commit v6 on v4

--- a/solution.py
+++ b/solution.py
@@ -59,7 +59,7 @@
     return items[0]
 
 
-def inverse_factor(gram_rows, midway):
+def inverse_factor(gram_rows):
     shape = (8, LANE)
     row8 = lax.broadcasted_iota(jnp.int32, shape, 0)
     lane = lax.broadcasted_iota(jnp.int32, shape, 1)
@@ -67,8 +67,6 @@
     inv = [jnp.where(lane % 32 == row8 + 8 * q, F32(1), F32(0)) for q in range(4)]
     out = []
     for p in range(4):
-        if p == 2:
-            midway()
         cols = [[jnp.broadcast_to(g[q][:, 8 * p + k : 8 * p + k + 1], shape) for q in range(p, 4)] for k in range(8)]
         diag = jnp.ones(shape, F32)
         for j in range(8):
@@ -231,10 +229,24 @@
 
     before, after = 4, 5
     along = [
-        remote(xbuf.at[jnp.where(x >= 2, before, after)], xbuf.at[8], row_send.at[2], row_recv.at[2], across),
+        remote(
+            xbuf.at[jnp.where(x >= 2, before, after), pl.ds(half, half)],
+            xbuf.at[8, pl.ds(half, half)],
+            row_send.at[2],
+            row_recv.at[2],
+            across,
+        ),
         remote(xbuf.at[jnp.where(x == 3, before, after)], xbuf.at[6], row_send.at[0], row_recv.at[0], right),
         remote(xbuf.at[jnp.where(x >= 1, before, after)], xbuf.at[7], row_send.at[1], row_recv.at[1], left),
     ]
+    same_x = tuple(jnp.where(x < 2, a, b) for a, b in zip(following, preceding))
+    over = remote(
+        xbuf.at[3, pl.ds(0, half)], xbuf.at[8, pl.ds(0, half)], row_send.at[3], row_recv.at[3], same_x
+    )
+
+    def row_arrived(k, block, part=None):
+        ref = xbuf.at[block] if part is None else xbuf.at[block, part]
+        pltpu.make_async_copy(ref, ref, row_recv.at[k]).wait()
 
     row8 = lax.broadcasted_iota(jnp.int32, (count, 8 * count), 0)
     lane8 = lax.broadcasted_iota(jnp.int32, (count, 8 * count), 1)
@@ -318,17 +330,20 @@
         current[...] = updated
         xbuf[0] = updated.astype(BF16)
         acc[...] = product(0) + product(4) + product(5)
-        xbuf[1] = orthonormal(images[parity, 1]).astype(BF16)
-        xbuf[2] = orthonormal(images[parity, 2]).astype(BF16)
-        acc[...] += product(1) + product(2)
         arrived(parity, 4, 3, pl.ds(0, half))
         arrived(parity, 5, 3, pl.ds(half, half))
         xbuf[3] = orthonormal(images[parity, 3]).astype(BF16)
-        acc[...] += product(3)
-        for k, block in ((0, 6), (1, 7), (2, 8)):
-            pltpu.make_async_copy(xbuf.at[block], xbuf.at[block], row_recv.at[k]).wait()
-        acc[...] += product(6) + product(7) + product(8)
-        for copy in spread(parity) + onward(parity) + along:
+        over.start()
+        xbuf[1] = orthonormal(images[parity, 1]).astype(BF16)
+        xbuf[2] = orthonormal(images[parity, 2]).astype(BF16)
+        acc[...] += product(1) + product(2) + product(3)
+        row_arrived(0, 6)
+        row_arrived(1, 7)
+        acc[...] += product(6) + product(7)
+        row_arrived(2, 8, pl.ds(half, half))
+        row_arrived(3, 8, pl.ds(0, half))
+        acc[...] += product(8)
+        for copy in spread(parity) + onward(parity) + along + [over]:
             copy.wait_send()
 
         image = stay_ref[...] * current[...] + scale_ref[...] * acc[...]
@@ -337,16 +352,11 @@
         base = parity * stages
         early = spread(1 - parity)
 
+        send_all(0, base, packed_product(pieces, pieces))
+
         @pl.when(jnp.logical_not(final))
         def _():
-            for copy in early[:2]:
-                copy.start()
-
-        send_all(0, base, packed_product(pieces, pieces))
-
-        @pl.when(jnp.logical_not(final))
-        def _():
-            for copy in early[2:]:
+            for copy in early:
                 copy.start()
 
         @pl.when(final)
@@ -362,18 +372,17 @@
 
         gram = unpacked(received(stages - 1, base))
 
-        def pass_on():
-            @pl.when(jnp.logical_not(final))
-            def _():
-                arrived(1 - parity, 2, 1)
-                arrived(1 - parity, 3, 2)
-                for copy in onward(1 - parity):
-                    copy.start()
+        @pl.when(jnp.logical_not(final))
+        def _():
+            arrived(1 - parity, 2, 1)
+            arrived(1 - parity, 3, 2)
+            for copy in onward(1 - parity):
+                copy.start()
 
         for stage in range(stages):
             wait_all(stage, base, sum_send)
 
-        high, mid, low = (piece.astype(F32) for piece in split3(inverse_factor(gram, pass_on)))
+        high, mid, low = (piece.astype(F32) for piece in split3(inverse_factor(gram)))
         left_a = jnp.where(lane32 < 2, high, mid)
         left_b = jnp.where(lane32 == 0, high, jnp.where(lane32 == 2, mid, low))
         left_ref[...] = jnp.concatenate([left_a, left_b], axis=1).astype(BF16)
@@ -443,8 +452,8 @@
             pltpu.VMEM((3 * len(PHASES), most, 8, LANE), F32),
             pltpu.SemaphoreType.DMA((6,)),
             pltpu.SemaphoreType.DMA((2, 6)),
-            pltpu.SemaphoreType.DMA((3,)),
-            pltpu.SemaphoreType.DMA((3,)),
+            pltpu.SemaphoreType.DMA((4,)),
+            pltpu.SemaphoreType.DMA((4,)),
             pltpu.SemaphoreType.DMA((3 * len(PHASES),)),
             pltpu.SemaphoreType.DMA((3 * len(PHASES),)),
             pltpu.SemaphoreType.DMA((2,)),

time: 275 us -> 237 us (0.86)
  Pallas kernels: 273 us -> 235 us
    pallas_call x1, Pallas kernels: 260 us -> 222 us  [shards(): pl.pallas_call(kernel, out_shape=(jax.ShapeDtypeStruct((count, rows), F32...]
where the time goes in v6:
time: 237 us; the launch traced here: 236 us
  Pallas kernels  235 us (99%)
    pallas_call x1, Pallas kernels, shards(): pl.pallas_call(kernel, out_shape=(jax.ShapeDtypeStruct((count, rows), F32...  222 us
    pallas_call x1, Pallas kernels, shards(): pl.pallas_call(align, out_shape=pltpu.VMEM((window * rows, rows), BF16),...  10 us

profile of v6, /device:TPU:1, one launch (start us, length us, event | category | flops | bytes accessed | tf_op | source)
XLA Modules:
  0.0 236.4 jit_solution(4422376533428059189)
XLA Ops:
  0.6 10.0 %align.1.weights = bf16[9216,1024]{1,0:T(8,128)(2,1)S(1)} custom-call(s32[4]{0:T(128)} %start_ref.2, s32[4]{0:T(128)} %width_ref.1, bf16[1024,8192]{1,0:T(8,128)(2,1)} %band_ref.1), custom_call_target="tpu_custom_call" | custom-call | tf_op jit(solution)/shard_map/align/pallas_call | solution.py:415
  10.7 2.5 %row_sums.1.rowsum_ref = f32[1,1024]{1,0:T(1,128)S(1)} custom-call(bf16[9216,1024]{1,0:T(8,128)(2,1)S(1)} %align.1.weights), custom_call_target="tpu_custom_call" | custom-call | tf_op jit(solution)/shard_map/row_sums/pallas_call | solution.py:431
  13.2 222.0 %subspace.1 = (f32[32,1024]{1,0:T(8,128)S(1)}, f32[32,32]{1,0:T(8,128)S(1)}) custom-call(f32[32,1024]{1,0:T(8,128)} %start_ref.3, f32[1,1024]{1,0:T(1,128)} %bitcast.1, f32[1,1024]{1,0:T(1,128)S(1)} %row_sums.1.rowsum_ref, bf16[9216,1024]{1,0:T(8,128)(2,1)S(1)} %align.1.weights), custom_call_target="tpu_custom_call" | custom-call | tf_op jit(solution)/shard_map/subspace/pallas_call | solution.py:439
  235.2 0.7 copy.9
  235.8 0.6 copy.10

commit v7 on v2

--- a/solution.py
+++ b/solution.py
@@ -90,19 +90,36 @@
     return jnp.concatenate(out, axis=0)
 
 
-def align(first_ref, width_ref, band_ref, weights, raw, sem):
+def align(start_ref, width_ref, band_ref, weights, raw, starts, widths, sem, small_sem):
     blocks, block_rows = raw.shape[0], raw.shape[1]
-    window = weights.shape[0]
-    loads = []
-    for b in range(blocks):
-        load = pltpu.make_async_copy(band_ref.at[pl.ds(b * block_rows, block_rows), :], raw.at[b], sem.at[b])
+    window, rows = weights.shape
+    chain = lax.axis_index("grp") * lax.axis_size("st") + lax.axis_index("st")
+    ahead, pieces = 2, 2
+    part = block_rows // pieces
+    loads = [
+        pltpu.make_async_copy(
+            band_ref.at[pl.ds(k * part, part), :], raw.at[k // pieces, pl.ds((k % pieces) * part, part)], sem.at[k]
+        )
+        for k in range(blocks * pieces)
+    ]
+    for load in loads[:ahead]:
         load.start()
-        loads.append(load)
+    small = [
+        pltpu.make_async_copy(start_ref, starts, small_sem.at[0]),
+        pltpu.make_async_copy(width_ref, widths, small_sem.at[1]),
+    ]
+    for copy in small:
+        copy.start()
+    for copy in small:
+        copy.wait()
     for b in range(blocks):
         here = slice(b * block_rows, (b + 1) * block_rows)
-        loads[b].wait()
-        first = first_ref[b] // LANE
-        used = width_ref[b] // LANE
+        for k in range(b * pieces, (b + 1) * pieces):
+            loads[k].wait()
+            if k + ahead < len(loads):
+                loads[k + ahead].start()
+        first = (starts[b] - chain * rows) // LANE + (window - rows) // (2 * LANE)
+        used = widths[b] // LANE
 
         def clear(e, carry, here=here):
             weights[pl.ds(pl.multiple_of(e * LANE, LANE), LANE), here] = jnp.zeros((LANE, block_rows), BF16)
@@ -300,14 +317,14 @@
         for k, block in ((0, 6), (1, 7), (2, 8)):
             pltpu.make_async_copy(xbuf.at[block], xbuf.at[block], row_recv.at[k]).wait()
         acc[...] += product(6) + product(7) + product(8)
-        for copy in spread(parity) + onward(parity) + along:
-            copy.wait_send()
-
         image = stay_ref[...] * current[...] + scale_ref[...] * acc[...]
         images[1 - parity, 0] = image
         pieces = split3(image)
         base = parity * stages
-        send_all(0, base, packed_product(pieces, pieces))
+        tile = packed_product(pieces, pieces)
+        for copy in spread(parity) + onward(parity) + along:
+            copy.wait_send()
+        send_all(0, base, tile)
 
         @pl.when(jnp.logical_not(final))
         def _():
@@ -324,8 +341,6 @@
             @pl.when(final)
             def _(stage=stage):
                 send_all(stage, cross, received(stage - 1, cross))
-
-        gram = unpacked(received(stages - 1, base))
 
         @pl.when(jnp.logical_not(final))
         def _():
@@ -334,13 +349,13 @@
             for copy in onward(1 - parity):
                 copy.start()
 
-        for stage in range(stages):
-            wait_all(stage, base, sum_send)
-
+        gram = unpacked(received(stages - 1, base))
         high, mid, low = (piece.astype(F32) for piece in split3(inverse_factor(gram)))
         left_a = jnp.where(lane32 < 2, high, mid)
         left_b = jnp.where(lane32 == 0, high, jnp.where(lane32 == 2, mid, low))
         left_ref[...] = jnp.concatenate([left_a, left_b], axis=1).astype(BF16)
+        for stage in range(stages):
+            wait_all(stage, base, sum_send)
         return carry
 
     lax.fori_loop(0, ITERS, one_step, 0)
@@ -360,20 +375,28 @@
     reach = span // (2 * rows)
     window = 2 * reach + 1
     vmem = pl.BlockSpec(memory_space=pltpu.VMEM)
-    smem = pl.BlockSpec(memory_space=pltpu.SMEM)
     most = max(math.prod(SIZES[name] for name in names) for names in PHASES)
     stay = stay.reshape(1, rows)
-    chain = lax.axis_index("grp") * lax.axis_size("st") + lax.axis_index("st")
-    first = band_start - (chain - reach) * rows
+    hbm = pl.BlockSpec(memory_space=pl.ANY)
+
+    def held(array):
+        return pltpu.with_memory_space_constraint(array, pltpu.HBM)
+
     weights = pl.pallas_call(
         align,
         out_shape=pltpu.VMEM((window * rows, rows), BF16),
-        in_specs=[smem, smem, pl.BlockSpec(memory_space=pl.ANY)],
+        in_specs=[hbm, hbm, hbm],
         out_specs=vmem,
-        scratch_shapes=[pltpu.VMEM((blocks, rows // blocks, span), BF16), pltpu.SemaphoreType.DMA((blocks,))],
+        scratch_shapes=[
+            pltpu.VMEM((blocks, rows // blocks, span), BF16),
+            pltpu.SMEM((blocks,), jnp.int32),
+            pltpu.SMEM((blocks,), jnp.int32),
+            pltpu.SemaphoreType.DMA((2 * blocks,)),
+            pltpu.SemaphoreType.DMA((2,)),
+        ],
         compiler_params=pltpu.CompilerParams(vmem_limit_bytes=24 * 1024 * 1024),
         name="align",
-    )(first, band_width, pltpu.with_memory_space_constraint(band_blocks, pltpu.HBM))
+    )(held(band_start), held(band_width), held(band_blocks))
     weights = pltpu.with_memory_space_constraint(weights, pltpu.VMEM)
     scale = pl.pallas_call(
         row_scale,

time: 234 us -> 229 us (0.979)
  Pallas kernels: 231 us -> 227 us
    pallas_call x1, Pallas kernels: 218 us -> 215 us  [shards(): pl.pallas_call(kernel, out_shape=(jax.ShapeDtypeStruct((count, rows), F32...]
where the time goes in v7:
time: 229 us
  Pallas kernels  227 us (99%)
    pallas_call x1, Pallas kernels, shards(): pl.pallas_call(kernel, out_shape=(jax.ShapeDtypeStruct((count, rows), F32...  215 us
    pallas_call x1, Pallas kernels, shards(): pl.pallas_call(align, out_shape=pltpu.VMEM((window * rows, rows), BF16),...  9.84 us

profile of v7, /device:TPU:1, one launch (start us, length us, event | category | flops | bytes accessed | tf_op | source)
XLA Modules:
  0.0 229.4 jit_solution(13155949943055300914)
XLA Ops:
  0.6 0.0 copy-start.1
  0.6 0.0 copy-start
  0.7 9.8 %align.1.weights = bf16[9216,1024]{1,0:T(8,128)(2,1)S(1)} custom-call(s32[4]{0:T(128)} %start_ref.2, s32[4]{0:T(128)} %width_ref.1, bf16[1024,8192]{1,0:T(8,128)(2,1)} %band_ref.1), custom_call_target="tpu_custom_call" | custom-call | tf_op jit(solution)/shard_map/align/pallas_call | solution.py:385
  10.5 0.0 copy-done.1
  10.5 2.5 %row_scale.1.scale_ref = f32[1,1024]{1,0:T(1,128)S(1)} custom-call(f32[1,1024]{1,0:T(1,128)S(1)} %bitcast.1, bf16[9216,1024]{1,0:T(8,128)(2,1)S(1)} %align.1.weights), custom_call_target="tpu_custom_call" | custom-call | tf_op jit(solution)/shard_map/row_scale/pallas_call | solution.py:401
  13.1 0.0 copy-done
  13.1 215.0 %subspace.1 = (f32[32,1024]{1,0:T(8,128)S(1)}, f32[32,32]{1,0:T(8,128)S(1)}) custom-call(f32[32,1024]{1,0:T(8,128)S(1)} %copy-done, f32[1,1024]{1,0:T(1,128)S(1)} %bitcast.2, f32[1,1024]{1,0:T(1,128)S(1)} %row_scale.1.scale_ref, bf16[9216,1024]{1,0:T(8,128)(2,1)S(1)} %align.1.weights), custom_call_target="tpu_custom_call" | custom-call | tf_op jit(solution)/shard_map/subspace/pallas_call | solution.py:409
  228.1 0.7 copy.9
  228.7 0.6 copy.10
Async XLA Ops:
  0.6 9.9 %copy-start.1 = (f32[1024]{0:T(1024)S(1)}, f32[1024]{0:T(1024)}, u32[]{:S(2)}) copy-start(f32[1024]{0:T(1024)} %param.6) | copy-start | bytes 12292
  0.6 12.4 %copy-start = (f32[32,1024]{1,0:T(8,128)S(1)}, f32[32,1024]{1,0:T(8,128)}, u32[]{:S(2)}) copy-start(f32[32,1024]{1,0:T(8,128)} %start_ref.3) | copy-start | bytes 393220

commit v8 on v7

--- a/solution.py
+++ b/solution.py
@@ -201,7 +201,7 @@
     def spread(parity):
         return [
             remote(images.at[parity, 0], images.at[parity, to], bulk_send.at[k], bulk_recv.at[parity, k], device)
-            for k, to, device in ((0, 4, following), (1, 5, preceding), (2, 1, right), (3, 2, left))
+            for k, to, device in ((2, 1, right), (3, 2, left), (0, 4, following), (1, 5, preceding))
         ]
 
     def onward(parity):

time: 229 us -> 230 us (level)
  no operation moved by 1% of the time
where the time goes in v8:
time: 230 us
  Pallas kernels  228 us (99%)
    pallas_call x1, Pallas kernels, shards(): pl.pallas_call(kernel, out_shape=(jax.ShapeDtypeStruct((count, rows), F32...  215 us
    pallas_call x1, Pallas kernels, shards(): pl.pallas_call(align, out_shape=pltpu.VMEM((window * rows, rows), BF16),...  10.1 us

profile of v8, /device:TPU:1, one launch (start us, length us, event | category | flops | bytes accessed | tf_op | source)
XLA Modules:
  0.0 229.5 jit_solution(8547487666698756502)
XLA Ops:
  0.6 0.0 copy-start.1
  0.6 0.0 copy-start
  0.7 10.1 %align.1.weights = bf16[9216,1024]{1,0:T(8,128)(2,1)S(1)} custom-call(s32[4]{0:T(128)} %start_ref.2, s32[4]{0:T(128)} %width_ref.1, bf16[1024,8192]{1,0:T(8,128)(2,1)} %band_ref.1), custom_call_target="tpu_custom_call" | custom-call | tf_op jit(solution)/shard_map/align/pallas_call | solution.py:385
  10.7 0.0 copy-done.1
  10.8 2.5 %row_scale.1.scale_ref = f32[1,1024]{1,0:T(1,128)S(1)} custom-call(f32[1,1024]{1,0:T(1,128)S(1)} %bitcast.1, bf16[9216,1024]{1,0:T(8,128)(2,1)S(1)} %align.1.weights), custom_call_target="tpu_custom_call" | custom-call | tf_op jit(solution)/shard_map/row_scale/pallas_call | solution.py:401
  13.3 0.0 copy-done
  13.3 214.9 %subspace.1 = (f32[32,1024]{1,0:T(8,128)S(1)}, f32[32,32]{1,0:T(8,128)S(1)}) custom-call(f32[32,1024]{1,0:T(8,128)S(1)} %copy-done, f32[1,1024]{1,0:T(1,128)S(1)} %bitcast.2, f32[1,1024]{1,0:T(1,128)S(1)} %row_scale.1.scale_ref, bf16[9216,1024]{1,0:T(8,128)(2,1)S(1)} %align.1.weights), custom_call_target="tpu_custom_call" | custom-call | tf_op jit(solution)/shard_map/subspace/pallas_call | solution.py:409
  228.2 0.7 copy.9
  228.9 0.6 copy.10
Async XLA Ops:
  0.6 10.1 %copy-start.1 = (f32[1024]{0:T(1024)S(1)}, f32[1024]{0:T(1024)}, u32[]{:S(2)}) copy-start(f32[1024]{0:T(1024)} %param.6) | copy-start | bytes 12292
  0.6 12.7 %copy-start = (f32[32,1024]{1,0:T(8,128)S(1)}, f32[32,1024]{1,0:T(8,128)}, u32[]{:S(2)}) copy-start(f32[32,1024]{1,0:T(8,128)} %start_ref.3) | copy-start | bytes 393220

commit v9 on v7

--- a/solution.py
+++ b/solution.py
@@ -130,7 +130,7 @@
             weights[pl.ds(pl.multiple_of((first + e) * LANE, LANE), LANE), here] = jnp.transpose(piece)
             return carry
 
-        lax.fori_loop(0, raw.shape[2] // LANE, turn, 0, unroll=8)
+        lax.fori_loop(0, raw.shape[2] // LANE, turn, 0, unroll=16)
         lax.fori_loop(0, first, clear, 0)
         lax.fori_loop(first + used, window // LANE, clear, 0)
 
@@ -298,8 +298,8 @@
         parity = t % 2
         final = t == ITERS - 1
         arrived(parity, 0, 4)
+        arrived(parity, 1, 5)
         xbuf[4] = orthonormal(images[parity, 4]).astype(BF16)
-        arrived(parity, 1, 5)
         xbuf[5] = orthonormal(images[parity, 5]).astype(BF16)
         for copy in along:
             copy.start()

time: 229 us -> 228 us (level)
  no operation moved by 1% of the time
where the time goes in v9:
time: 228 us
  Pallas kernels  226 us (99%)
    pallas_call x1, Pallas kernels, shards(): pl.pallas_call(kernel, out_shape=(jax.ShapeDtypeStruct((count, rows), F32...  214 us
    pallas_call x1, Pallas kernels, shards(): pl.pallas_call(align, out_shape=pltpu.VMEM((window * rows, rows), BF16),...  9.39 us

profile of v9, /device:TPU:1, one launch (start us, length us, event | category | flops | bytes accessed | tf_op | source)
XLA Modules:
  0.0 227.9 jit_solution(7181996346837633539)
XLA Ops:
  0.6 0.0 copy-start.1
  0.6 0.0 copy-start
  0.7 9.4 %align.1.weights = bf16[9216,1024]{1,0:T(8,128)(2,1)S(1)} custom-call(s32[4]{0:T(128)} %start_ref.2, s32[4]{0:T(128)} %width_ref.1, bf16[1024,8192]{1,0:T(8,128)(2,1)} %band_ref.1), custom_call_target="tpu_custom_call" | custom-call | tf_op jit(solution)/shard_map/align/pallas_call | solution.py:385
  10.0 0.0 copy-done.1
  10.1 2.5 %row_scale.1.scale_ref = f32[1,1024]{1,0:T(1,128)S(1)} custom-call(f32[1,1024]{1,0:T(1,128)S(1)} %bitcast.1, bf16[9216,1024]{1,0:T(8,128)(2,1)S(1)} %align.1.weights), custom_call_target="tpu_custom_call" | custom-call | tf_op jit(solution)/shard_map/row_scale/pallas_call | solution.py:401
  12.6 0.0 copy-done
  12.6 214.1 %subspace.1 = (f32[32,1024]{1,0:T(8,128)S(1)}, f32[32,32]{1,0:T(8,128)S(1)}) custom-call(f32[32,1024]{1,0:T(8,128)S(1)} %copy-done, f32[1,1024]{1,0:T(1,128)S(1)} %bitcast.2, f32[1,1024]{1,0:T(1,128)S(1)} %row_scale.1.scale_ref, bf16[9216,1024]{1,0:T(8,128)(2,1)S(1)} %align.1.weights), custom_call_target="tpu_custom_call" | custom-call | tf_op jit(solution)/shard_map/subspace/pallas_call | solution.py:409
  226.7 0.7 copy.9
  227.3 0.6 copy.10
Async XLA Ops:
  0.6 9.4 %copy-start.1 = (f32[1024]{0:T(1024)S(1)}, f32[1024]{0:T(1024)}, u32[]{:S(2)}) copy-start(f32[1024]{0:T(1024)} %param.6) | copy-start | bytes 12292
  0.6 12.0 %copy-start = (f32[32,1024]{1,0:T(8,128)S(1)}, f32[32,1024]{1,0:T(8,128)}, u32[]{:S(2)}) copy-start(f32[32,1024]{1,0:T(8,128)} %start_ref.3) | copy-start | bytes 393220
